TPU v7x, 512 devices: a whole 4x8x8 slice. The times are simulated.
512 devices in a mesh: ctx: 32 (over z, x), ch: 16 (over y, core).
Axes of the slice: x: 4, y: 8, z: 8, core: 2. Of those that a mesh axis runs over, the one named last changes fastest.
Arguments:
- gate_outer: bfloat16 [4096, 4096], P('ctx', 'ch'), may hold values from -70 to 70
- gate_inner: bfloat16 [4096, 4096], P('ctx', 'ch'), may hold values from -6 to 6
- conv_input: bfloat16 [4096, 4096], P('ctx', 'ch'), may hold values from -6 to 6
- filters: bfloat16 [256, 128], P('ch'), may hold values from -0.5 to 0.5
- queries: bfloat16 [4096, 4096], P('ctx', 'ch'), may hold values from -5.5 to 5.5
- keys: bfloat16 [4096, 4096], P('ctx', 'ch'), may hold values from -5.5 to 5.5
- cotangent: bfloat16 [4096, 4096], P('ctx', 'ch'), may hold values from -6 to 6
Outputs:
- attended: bfloat16 [4096, 4096], P('ctx', 'ch')
- grad_query: bfloat16 [4096, 4096], P('ctx', 'ch')
- grad_key: bfloat16 [4096, 4096], P('ctx', 'ch')
- grad_gate_outer: bfloat16 [4096, 4096], P('ctx', 'ch')
- grad_filters: float32 [256, 128], P('ch')
All inputs are finite; a program needn't handle non-finite values.
Results may differ from a plain program's by a relative error of at most 0.012.
The roundings to bfloat16 on the way count: a program that leaves them out, or rounds other values in their place, can miss the bound.
Values may be sent and summed in bfloat16 or wider, within the bound.
A program may use at most 64 MiB of HBM per device.

v0:
```python
import math

import jax
import jax.numpy as jnp
from jax import lax
from jax.sharding import PartitionSpec as P

HEAD_DIM = 128


NEGATIVE = -1e30
EPSILON = 1e-05


def from_behind(array, axis, by):
    size = lax.axis_size(axis)
    pairs = [(i, i + by) for i in range(size) if 0 <= i + by < size]
    return lax.ppermute(array, axis, pairs)


def channel_total(partial_value):
    return lax.psum(partial_value, "ch")


def in_blocks(step, state_in, pieces):
    row_span = pieces[0].shape[0]
    block_rows = 512
    block_total = row_span // block_rows

    def one_block(block_index, running):
        offset = block_index * block_rows
        sliced = tuple(
            (lax.dynamic_slice_in_dim(member, offset, block_rows, 0) for member in pieces)
        )
        return step(running, sliced, offset)

    return lax.fori_loop(0, block_total, one_block, state_in)


def on_device(gate_outer, gate_inner, conv_input, filters, queries, keys, cotangent):
    tok_rows, chan_count = gate_outer.shape
    group_count, tap_count = filters.shape
    group_size = chan_count // group_count
    head_count = chan_count // HEAD_DIM
    score_scale = 1.0 / math.sqrt(HEAD_DIM)
    total_width = chan_count * lax.axis_size("ch")
    own_index = lax.axis_index("ctx")
    row_start = own_index * tok_rows
    positions = row_start + jnp.arange(tok_rows, dtype=jnp.int32)
    product = (gate_inner.astype(jnp.float32) * conv_input.astype(jnp.float32)).astype(jnp.bfloat16)
    lower_rim = from_behind(product[tok_rows - tap_count + 1 :], "ctx", 1)
    padded = jnp.concatenate([jnp.zeros((1, chan_count), jnp.bfloat16), lower_rim, product], axis=0)
    blocks = padded.reshape(tok_rows // tap_count + 1, tap_count, group_count, group_size)
    windows = jnp.concatenate([blocks[:-1], blocks[1:]], axis=1)
    tap_table = jnp.arange(tap_count)[:, None] + tap_count - jnp.arange(2 * tap_count)[None, :]
    inside = (tap_table >= 0) & (tap_table < tap_count)
    toeplitz = jnp.where(
        inside[None], filters[:, jnp.clip(tap_table, 0, tap_count - 1)], jnp.zeros((), jnp.bfloat16)
    )
    conv_out = jnp.einsum(
        "gts,bsgc->btgc", toeplitz, windows, preferred_element_type=jnp.float32
    ).reshape(tok_rows, chan_count)
    mixer = gate_outer.astype(jnp.float32) * conv_out
    inv_rms = lax.rsqrt(channel_total(jnp.sum(mixer * mixer, axis=1)) / total_width + EPSILON)
    values = (mixer * inv_rms[:, None]).astype(jnp.bfloat16)

    def split_rows(matrix):
        return matrix.reshape(matrix.shape[0], head_count, HEAD_DIM)

    query_heads = split_rows(queries)
    key_heads = split_rows(keys)
    value_heads = split_rows(values)
    cot_heads = split_rows(cotangent)

    def query_scores(key_block, row_from):
        row_span = key_block.shape[0]
        scores = (
            jnp.einsum(
                "thd,shd->hts",
                query_heads,
                split_rows(key_block),
                preferred_element_type=jnp.float32,
            )
            * score_scale
        )
        allowed = (positions[:, None] >= row_from + jnp.arange(row_span, dtype=jnp.int32)[None, :])[
            None
        ]
        return (jnp.where(allowed, scores, NEGATIVE), allowed)

    def stat_step(state_in, pieces, row_from):
        run_top, run_total = state_in
        masked, allowed = query_scores(pieces[0], row_from)
        new_top = jnp.maximum(run_top, jnp.max(masked, axis=2))
        fresh = jnp.where(allowed, jnp.exp(masked - new_top[:, :, None]), 0.0)
        return (new_top, run_total * jnp.exp(run_top - new_top) + jnp.sum(fresh, axis=2))

    stat_init = (
        jnp.full((head_count, tok_rows), NEGATIVE, jnp.float32),
        jnp.zeros((head_count, tok_rows), jnp.float32),
    )
    zero_grad = jnp.zeros((tok_rows, head_count, HEAD_DIM), jnp.float32)

    def value_step(state_in, pieces, row_from):
        masked, allowed = query_scores(pieces[0], row_from)
        prob_low = jnp.where(allowed, jnp.exp(masked - log_total[:, :, None]), 0.0).astype(
            jnp.bfloat16
        )
        return state_in + jnp.einsum(
            "hts,shd->thd", prob_low, split_rows(pieces[1]), preferred_element_type=jnp.float32
        )

    run_top, run_total = in_blocks(
        stat_step, stat_init, (lax.all_gather(keys, "ctx", axis=0, tiled=True),)
    )
    log_total = run_top + jnp.log(run_total)
    totals = in_blocks(
        value_step,
        zero_grad,
        (
            lax.all_gather(keys, "ctx", axis=0, tiled=True),
            lax.all_gather(values, "ctx", axis=0, tiled=True),
        ),
    )
    attended = totals.reshape(tok_rows, chan_count).astype(jnp.bfloat16)
    attended_wide = lax.optimization_barrier(attended).astype(jnp.float32)
    row_delta = jnp.sum(cot_heads.astype(jnp.float32) * split_rows(attended_wide), axis=2).T

    def key_terms(query_block, cot_block, top_block, delta_block, row_from):
        row_span = query_block.shape[0]
        block_query = split_rows(query_block)
        block_cot = split_rows(cot_block)
        scores = (
            jnp.einsum("shd,thd->hst", block_query, key_heads, preferred_element_type=jnp.float32)
            * score_scale
        )
        allowed = (
            (row_from + jnp.arange(row_span, dtype=jnp.int32))[:, None] >= positions[None, :]
        )[None]
        weights = jnp.where(
            allowed, jnp.exp(jnp.where(allowed, scores, NEGATIVE) - top_block[:, :, None]), 0.0
        )
        prob_grad = jnp.einsum(
            "shd,thd->hst", block_cot, value_heads, preferred_element_type=jnp.float32
        )
        score_grad = (weights * (prob_grad - delta_block[:, :, None])).astype(jnp.bfloat16)
        return (score_grad, weights.astype(jnp.bfloat16), block_query, block_cot)

    def grad_step(state_in, pieces, row_from):
        masked, allowed = query_scores(pieces[0], row_from)
        weights = jnp.where(allowed, jnp.exp(masked - log_total[:, :, None]), 0.0)
        prob_grad = jnp.einsum(
            "thd,shd->hts", cot_heads, split_rows(pieces[1]), preferred_element_type=jnp.float32
        )
        score_grad = (weights * (prob_grad - row_delta[:, :, None])).astype(jnp.bfloat16)
        return state_in + jnp.einsum(
            "hts,shd->thd", score_grad, split_rows(pieces[0]), preferred_element_type=jnp.float32
        )

    query_grad = in_blocks(
        grad_step,
        zero_grad,
        (
            lax.all_gather(keys, "ctx", axis=0, tiled=True),
            lax.all_gather(values, "ctx", axis=0, tiled=True),
        ),
    )
    top_all, delta_all = (
        lax.all_gather(log_total.T, "ctx", axis=0, tiled=True),
        lax.all_gather(row_delta.T, "ctx", axis=0, tiled=True),
    )

    def key_step(state_in, pieces, row_from):
        row_span = pieces[0].shape[0]
        key_now, value_now = state_in
        top_block = lax.dynamic_slice_in_dim(top_all, row_from, row_span, 0).T
        delta_block = lax.dynamic_slice_in_dim(delta_all, row_from, row_span, 0).T
        score_grad, prob_low, block_query, block_cot = key_terms(
            pieces[0], pieces[1], top_block, delta_block, row_from
        )
        return (
            key_now
            + jnp.einsum(
                "hst,shd->thd", score_grad, block_query, preferred_element_type=jnp.float32
            ),
            value_now
            + jnp.einsum("hst,shd->thd", prob_low, block_cot, preferred_element_type=jnp.float32),
        )

    key_grad, value_grad = in_blocks(
        key_step,
        (zero_grad, zero_grad),
        (
            lax.all_gather(queries, "ctx", axis=0, tiled=True),
            lax.all_gather(cotangent, "ctx", axis=0, tiled=True),
        ),
    )
    grad_query = (query_grad * score_scale).reshape(tok_rows, chan_count).astype(jnp.bfloat16)
    grad_key = (key_grad * score_scale).reshape(tok_rows, chan_count).astype(jnp.bfloat16)
    grad_values = value_grad.reshape(tok_rows, chan_count)
    projection = channel_total(jnp.sum(grad_values * mixer, axis=1))
    cube = inv_rms * inv_rms * inv_rms
    mixer_grad = inv_rms[:, None] * grad_values - mixer * (cube * projection / total_width)[:, None]
    grad_gate_outer = (mixer_grad * conv_out).astype(jnp.bfloat16)
    conv_grad = (mixer_grad * gate_outer.astype(jnp.float32)).astype(jnp.bfloat16)
    grad_blocks = conv_grad.reshape(tok_rows // tap_count, tap_count, group_count, group_size)
    pair_sums = jnp.einsum(
        "btgc,bsgc->gts", grad_blocks, windows, preferred_element_type=jnp.float32
    )
    flat_sums = jnp.pad(
        pair_sums.reshape(group_count, 2 * tap_count * tap_count), ((0, 0), (0, tap_count))
    )
    diagonal = flat_sums.reshape(group_count, tap_count, 2 * tap_count + 1).sum(axis=1)
    partial_grad = diagonal[:, tap_count:0:-1]
    grad_filters = lax.psum(partial_grad, "ctx")
    return (attended, grad_query, grad_key, grad_gate_outer, grad_filters)


def solution(mesh):
    placed = (
        P("ctx", "ch"),
        P("ctx", "ch"),
        P("ctx", "ch"),
        P("ch", None),
        P("ctx", "ch"),
        P("ctx", "ch"),
        P("ctx", "ch"),
    )
    return jax.shard_map(
        on_device,
        mesh=mesh,
        in_specs=placed,
        out_specs=(P("ctx", "ch"), P("ctx", "ch"), P("ctx", "ch"), P("ctx", "ch"), P("ch", None)),
        check_vma=False,
    )
```

profile of v0, /device:TPU:24, one launch (start us, length us, event | category | flops | bytes accessed | tf_op | source)
XLA Modules:
  0.0 549.4 jit_solution(15507215589830400794)
XLA Ops:
  7.2 1.6 copy.88
  9.8 3.4 collective-permute-start
  14.4 114.9 %gather_fusion = bf16[32768,16]{1,0:T(8,128)(2,1)} fusion(bf16[16,128]{0,1:T(8,128)(2,1)S(1)} %copy.86, s32[32768]{0:T(1024)S(1)} %broadcast_clamp_fusion), kind=kCustom, calls=%fused_computation | custom fusion | bytes 2228224 | tf_op jit(solution)/shard_map/gather | solution.py:58
  129.3 7.1 %copy.87 = bf16[128,256,16]{1,0,2:T(8,128)(2,1)S(1)} copy(bf16[128,256,16]{2,1,0:T(8,128)(2,1)} %bitcast.217) | data formatting | bytes 2097152 | tf_op jit(solution)/shard_map/gather | solution.py:58
  137.2 22.4 %psum.21 = f32[128]{0:T(128)S(1)} all-reduce(f32[128]{0:T(128)S(1)} %multiply_reduce_fusion.1), channel_id=1, replica_groups=mesh['ctx'=32,'ch'=16] {'ch'}, use_global_device_ids=true, to_apply=%region_1.2 | all-reduce | flops 128 | bytes 1024 | tf_op jit(solution)/shard_map/psum | solution.py:22
  165.0 13.1 %while.60 = (s32[]{:T(128)}, f32[2,128]{1,0:T(2,128)S(1)}, f32[2,128]{1,0:T(2,128)S(1)}, bf16[4096,256]{0,1:T(8,128)(2,1)}, bf16[128,2,128]{2,0,1:T(8,128)(2,1)S...) while((s32[]{:T(128)}, f32[2,128]{1,0:T(2,128)S(1)}, ...), condition=%wide.region_5.6_spmd.clone, body=%wide.region_2.5_spmd.clone.sunk | while | flops 34408324 | bytes 2115762 | solution.py:37
  178.2 48.7 %all_gather.24 = f32[4096,2]{0,1:T(2,128)S(1)} all-gather(f32[128,2]{0,1:T(2,128)S(1)} %bitcast.236), channel_id=1, replica_groups=mesh['ctx'=32,'ch'=16] {'ctx'}, dimensions={0}, use_global_device_ids=true | all-gather | bytes 33792 | tf_op jit(solution)/shard_map/all_gather | solution.py:169
  226.9 20.1 %all-gather.5.cloned.1.call-done = bf16[4096,256]{0,1:T(8,128)(2,1)} async-done(((bf16[128,256]{0,1:T(8,128)(2,1)}), bf16[4096,256]{0,1:T(8,128)(2,1)}) %all-gather.5.cloned.1.call-update) | async-done | bytes 2097168 | tf_op jit(solution)/shard_map/all_gather | solution.py:122
  246.9 14.3 %while.61 = (s32[]{:T(128)}, f32[128,2,128]{0,2,1:T(8,128)S(1)}, bf16[4096,256]{0,1:T(8,128)(2,1)}, bf16[4096,256]{0,1:T(8,128)(2,1)}, bf16[128,2,128]{2,0,1:T(8...) while((s32[]{:T(128)}, f32[128,2,128]{0,2,1:T(8,128)S(1)}, ...), condition=%wide.region_7.8_spmd.clone, body=%wide.region_6.7_spmd.clone.sunk | while | flops 67895944 | bytes 2037945 | solution.py:37
  246.9 1.1 constant_dynamic-slice_fusion.12
  248.7 1.1 constant_dynamic-slice_fusion.12
  250.5 1.1 constant_dynamic-slice_fusion.12
  252.3 1.1 constant_dynamic-slice_fusion.12
  262.0 16.7 %while.62 = (s32[]{:T(128)}, f32[128,2,128]{0,2,1:T(8,128)S(1)}, bf16[4096,256]{0,1:T(8,128)(2,1)}, bf16[128,2,128]{2,0,1:T(8,128)(2,1)S(1)}, f32[2,128]{1,0:T(2...) while((s32[]{:T(128)}, f32[128,2,128]{0,2,1:T(8,128)S(1)}, ...), condition=%wide.region_10.11_spmd.clone, body=%wide.region_9.10_spmd.clone.sunk | while | flops 101712512 | bytes 3415241 | solution.py:37
  264.1 1.1 constant_dynamic-slice_fusion.13
  279.5 52.6 %all_gather.26 = f32[4096,2]{1,0:T(8,128)S(1)} all-gather(f32[128,2]{1,0:T(8,128)S(1)} %copy.119), channel_id=1, replica_groups=mesh['ctx'=32,'ch'=16] {'ctx'}, dimensions={0}, use_global_device_ids=true | all-gather | bytes 33792 | tf_op jit(solution)/shard_map/all_gather | solution.py:170
  332.6 1.4 all-gather.9.cloned.1.call-done
  334.1 82.9 %all-gather.11.cloned.1.call-done = bf16[4096,256]{0,1:T(8,128)(2,1)} async-done(((bf16[128,256]{0,1:T(8,128)(2,1)}), bf16[4096,256]{0,1:T(8,128)(2,1)}) %all-gather.11.cloned.1.call-update) | async-done | bytes 2097168 | tf_op jit(solution)/shard_map/all_gather | solution.py:195
  417.0 18.9 %while.63 = (s32[]{:T(128)}, f32[128,2,128]{0,2,1:T(8,128)S(1)}, f32[128,2,128]{0,2,1:T(8,128)S(1)}, bf16[4096,256]{0,1:T(8,128)(2,1)}, bf16[128,2,128]{2,0,1:T(...) while((s32[]{:T(128)}, f32[128,2,128]{0,2,1:T(8,128)S(1)}, ...), condition=%wide.region_12.13_spmd.clone, body=%wide.region_11.12_spmd.clone.sunk | while | flops 135463552 | bytes 4486358 | solution.py:37
  436.7 22.3 %psum.22 = f32[128]{0:T(128)S(1)} all-reduce(f32[128]{0:T(128)S(1)} %fusion.62), channel_id=1, replica_groups=mesh['ctx'=32,'ch'=16] {'ch'}, use_global_device_ids=true, to_apply=%region_14.15 | all-reduce | flops 128 | bytes 1024 | tf_op jit(solution)/shard_map/psum | solution.py:22
  460.3 1.2 copy.122
  461.5 1.5 pad.5
  463.0 3.7 reshape.330
  467.1 75.8 %psum.23 = f32[16,128]{1,0:T(8,128)} all-reduce(f32[16,128]{1,0:T(8,128)S(1)} %rev.3), channel_id=1, replica_groups=mesh['ctx'=32,'ch'=16] {'ctx'}, use_global_device_ids=true, to_apply=%region_16.17 | all-reduce | flops 2048 | bytes 16384 | tf_op jit(solution)/shard_map/psum | solution.py:215
  (289 shorter events, 68.3 us)
Async XLA Ops:
  7.2 157.9 %all-gather.7.cloned.1.call-start = ((), (), s32[]{:S(2)}) async-start(), calls=%async_computation.1 | async-start | bytes 2162688 | tf_op jit(solution)/shard_map/all_gather | solution.py:121
  8.8 238.1 %all-gather.5.cloned.1.call-start = ((), (), s32[]{:S(2)}) async-start(), calls=%async_computation | async-start | bytes 2162688 | tf_op jit(solution)/shard_map/all_gather | solution.py:122
  9.8 126.8 %collective-permute-start = (bf16[127,256]{1,0:T(8,128)(2,1)S(1)}, bf16[127,256]{1,0:T(8,128)(2,1)S(1)}, u32[]{:S(2)}, u32[]{:S(2)}) collective-permute-start(bf16[127,256]{1,0:T(8,128)(2,1)S(1)} %slice.21), channel_id=1, source_target_pairs={{0,16},{16,32},{32,48},{48,64},{64,80},{80,96},{96,112},{112,128},... | collective-permute-start | bytes 195080 | tf_op jit(solution)/shard_map/ppermute | solution.py:18
  129.3 7.1 %copy-start.3 = (bf16[128,256]{1,0:T(8,128)(2,1)S(1)}, bf16[128,256]{1,0:T(8,128)(2,1)}, u32[]{:S(2)}) copy-start(bf16[128,256]{1,0:T(8,128)(2,1)} %param.15) | copy-start | bytes 196612
  136.4 24.0 %copy-start.4 = (bf16[128,256]{1,0:T(8,128)(2,1)S(1)}, bf16[128,256]{1,0:T(8,128)(2,1)}, u32[]{:S(2)}) copy-start(bf16[128,256]{1,0:T(8,128)(2,1)} %param.19) | copy-start | bytes 196612
  136.4 24.8 %copy-start.5 = (bf16[128,256]{1,0:T(8,128)(2,1)S(1)}, bf16[128,256]{1,0:T(8,128)(2,1)}, u32[]{:S(2)}) copy-start(bf16[128,256]{1,0:T(8,128)(2,1)} %param.21) | copy-start | bytes 196612
  136.4 27.5 %copy-start.1 = (bf16[128,256]{0,1:T(8,128)(2,1)S(1)}, bf16[128,256]{0,1:T(8,128)(2,1)}, u32[]{:S(2)}) copy-start(bf16[128,256]{0,1:T(8,128)(2,1)} %copy.88) | copy-start | bytes 196612
  160.3 173.8 %all-gather.9.cloned.1.call-start = ((), (), s32[]{:S(2)}) async-start(), calls=%async_computation.2 | async-start | bytes 2162688 | tf_op jit(solution)/shard_map/all_gather | solution.py:194
  161.1 255.8 %all-gather.11.cloned.1.call-start = ((), (), s32[]{:S(2)}) async-start(), calls=%async_computation.3 | async-start | bytes 2162688 | tf_op jit(solution)/shard_map/all_gather | solution.py:195
  246.9 14.6 %copy-start = (bf16[128,256]{0,1:T(8,128)(2,1)S(1)}, bf16[128,256]{0,1:T(8,128)(2,1)}, u32[]{:S(2)}) copy-start(bf16[128,256]{0,1:T(8,128)(2,1)} %copy.93) | copy-start | bytes 196612
  261.4 0.6 copy-start.2
Sparse Core Ops, SparseCore 0:
  11.6 85.5 all-gather.6
  160.4 86.4 all-gather.4
  250.0 84.0 all-gather.8
  337.0 79.9 all-gather.10
where the time goes:
time: 552 us; the launch traced here: 549 us
  blocking collectives  222 us (40%)
  local copies, waits for them, and re-layouts  173 us (31%)
  waiting for transfers between devices  104 us (19%)
  matrix products  22.4 us (4%)
  between operations  14.2 us (3%)
  other arithmetic  8 us (1%)
    gather x2, local copies, waits for them, and re-layouts, on_device(): filters[:, jnp.clip(tap_table, 0, tap_count - 1)]  122 us
    all_gather x1, waiting for transfers between devices, on_device(): lax.all_gather(cotangent, 'ctx', axis=0, tiled=True)  82.9 us
    psum x1, blocking collectives, on_device(): grad_filters = lax.psum(partial_grad, 'ctx')  75.8 us
    all_gather x1, blocking collectives, on_device(): lax.all_gather(row_delta.T, 'ctx', axis=0, tiled=True)  52.6 us
    all_gather x1, blocking collectives, on_device(): lax.all_gather(log_total.T, 'ctx', axis=0, tiled=True)  48.7 us
    psum x2, blocking collectives, channel_total(): return lax.psum(partial_value, 'ch')  44.7 us
    dynamic_slice x32, local copies, waits for them, and re-layouts, one_block(): lax.dynamic_slice_in_dim(member, offset, block_rows, 0)  33.5 us
    all_gather x1, waiting for transfers between devices, on_device(): lax.all_gather(values, 'ctx', axis=0, tiled=True)  20.1 us
  transfers between devices with their start and end apart: 5, of which 3 were waited for; matrix products, arithmetic and copies ran while one was open for 32% of the time, Pallas kernels for 0%

commit v1 on v0

v1 whole, which is shorter than its diff:
```python
import functools
import math

import jax
import jax.numpy as jnp
from jax import lax
from jax.experimental import pallas as pl
from jax.experimental.pallas import tpu as pltpu
from jax.sharding import PartitionSpec as P

MESH = pl.DeviceIdType.MESH
HEAD_DIM = 128
NEGATIVE = -1e30
EPSILON = 1e-05
NX = 4
NC = 2
F32 = jnp.float32
BF16 = jnp.bfloat16

NT = (((1,), (1,)), ((), ()))
NN = (((1,), (0,)), ((), ()))
TN = (((0,), (0,)), ((), ()))


def dot(a, b, dims):
    return lax.dot_general(a, b, dims, preferred_element_type=F32)


def kernel(
    NZ, NY,
    go, gi, ci, filt, q, k, cot,
    att_o, dq_o, dk_o, ggo_o, gf_o,
    k_all, v_all, q_all, c_all, win, toep, s_buf, dp_buf, p_low, ds_low,
    lse_buf, d_buf, core_buf, y_buf, fx_buf, fz_buf,
    dv_src, dv_buf, dk_src, dk_buf, att_src, att_buf, dq_src, dq_buf,
    mix_buf, conv_buf, win_back, lse_sum, delta_sum,
    ssem, rk, rv, rq, rc, rhalo, rlse, rd, rcore, ry, rdv, rdk, ratt, rdq, rfx, rfz,
):
    rows, chans = go.shape
    groups, taps = filt.shape
    group_size = chans // groups
    heads = chans // HEAD_DIM
    width = chans * NY * NC
    scale = 1.0 / math.sqrt(HEAD_DIM)
    ctx, ch = lax.axis_index("ctx"), lax.axis_index("ch")
    z, x = ctx // NX, ctx % NX
    y, core = ch // NC, ch % NC
    last = NZ * NX - 1

    def z_dev(zp):
        return (zp * NX + x, ch)

    def x_dev(xp):
        return (z * NX + xp, ch)

    def y_dev(yp):
        return (ctx, yp * NC + core)

    sibling = (ctx, y * NC + (1 - core))
    z_peer = [lax.rem(z + o, NZ) for o in range(NZ)]
    x_peer = [lax.rem(x + o, NX) for o in range(NX)]
    y_peer = [lax.rem(y + o, NY) for o in range(NY)]
    near = lambda n: [o for d in range(1, n // 2 + 1) for o in dict.fromkeys((d, n - d))]
    z_order, x_order, y_order = near(NZ), near(NX), near(NY)
    before = lax.rem(ctx + last, last + 1)
    after = lax.rem(ctx + 1, last + 1)

    sends = []

    def push(src, dst, recv_sem, dev):
        copy = pltpu.make_async_remote_copy(
            src_ref=src, dst_ref=dst, send_sem=ssem.at[len(sends)], recv_sem=recv_sem,
            device_id=dev, device_id_type=MESH,
        )
        sends.append(copy)
        copy.start()

    def arrive(dst, recv_sem, dev):
        pltpu.make_async_remote_copy(
            src_ref=dst, dst_ref=dst, send_sem=ssem.at[0], recv_sem=recv_sem,
            device_id=dev, device_id_type=MESH,
        ).wait_recv()

    barrier = pltpu.get_barrier_semaphore()
    greeted = 0
    for dev in (
        [z_dev(z_peer[o]) for o in z_order]
        + [x_dev(x_peer[o]) for o in x_order]
        + [y_dev(y_peer[o]) for o in y_order]
        + [sibling, (before, ch)]
    ):
        pl.semaphore_signal(barrier, inc=1, device_id=dev, device_id_type=MESH)
        greeted += 1

    x_rows = pl.ds(pl.multiple_of(x * rows, rows), rows)
    k_all[x_rows] = k[...]
    q_all[z] = q[...]
    c_all[z] = cot[...]
    win[rows:] = (gi[...].astype(F32) * ci[...].astype(F32)).astype(BF16)
    flip = (
        lax.broadcasted_iota(jnp.int32, (taps, 2 * taps), 0)
        + lax.broadcasted_iota(jnp.int32, (taps, 2 * taps), 1)
        == taps
    ).astype(F32).astype(BF16)
    turned = dot(filt[...], flip, NN)
    for g in range(groups):
        spread = jnp.broadcast_to(turned[g : g + 1], (rows, 2 * taps))
        spread = pltpu.roll(spread, 0, 1, stride=1, stride_axis=0)
        toep[g * rows : (g + 1) * rows] = spread.astype(BF16)

    pl.semaphore_wait(barrier, greeted)

    @pl.when(ctx < last)
    def _():
        pltpu.make_async_remote_copy(
            src_ref=win.at[pl.ds(rows, rows)], dst_ref=win.at[pl.ds(0, rows)],
            send_sem=ssem.at[ssem.shape[0] - 1], recv_sem=rhalo,
            device_id=(after, ch), device_id_type=MESH,
        ).start()

    for o in x_order:
        push(k, k_all.at[x_rows], rk.at[x], x_dev(x_peer[o]))
    for o in z_order:
        push(q, q_all.at[z], rq.at[z], z_dev(z_peer[o]))
    for o in z_order:
        push(cot, c_all.at[z], rc.at[z], z_dev(z_peer[o]))

    @pl.when(ctx > 0)
    def _():
        pltpu.make_async_remote_copy(
            src_ref=win.at[pl.ds(0, rows)], dst_ref=win.at[pl.ds(0, rows)],
            send_sem=ssem.at[0], recv_sem=rhalo, device_id=(before, ch), device_id_type=MESH,
        ).wait_recv()

    @pl.when(ctx == 0)
    def _():
        win[:rows] = jnp.zeros((rows, chans), BF16)

    lane_group = lax.broadcasted_iota(jnp.int32, (rows, chans), 1) // group_size
    window = win[...]
    conv = jnp.zeros((rows, chans), F32)
    for g in range(groups):
        part = dot(toep[g * rows : (g + 1) * rows], window, NN)
        conv = jnp.where(lane_group == g, part, conv)
    conv_buf[...] = conv
    back = (
        lax.broadcasted_iota(jnp.int32, (2 * rows, 2 * rows), 0)
        + lax.broadcasted_iota(jnp.int32, (2 * rows, 2 * rows), 1)
        == 2 * rows - 1
    ).astype(F32).astype(BF16)
    win_back[...] = dot(back, window, NN).astype(BF16)
    mixer = go[...].astype(F32) * conv
    mix_buf[...] = mixer

    def as_row(column):
        return jnp.broadcast_to(column, (rows, 128)).T[:8]

    def as_tile(row):
        tile = jnp.broadcast_to(row[0:1], (128, rows)).T
        return jnp.concatenate([tile] * (chans // 128), axis=1)

    def to_sibling(phase, column):
        core_buf[phase, core] = as_row(column)
        push(core_buf.at[phase, core], core_buf.at[phase, core], rcore.at[phase], sibling)

    def to_y(phase):
        arrive(core_buf.at[phase, 1 - core], rcore.at[phase], sibling)
        y_buf[phase, y] = core_buf[phase, 0] + core_buf[phase, 1]
        for o in y_order:
            push(y_buf.at[phase, y], y_buf.at[phase, y], ry.at[phase, y], y_dev(y_peer[o]))

    def from_y(phase):
        for o in y_order:
            arrive(y_buf.at[phase, y_peer[o]], ry.at[phase, y_peer[o]], y_dev(y_peer[o]))
        total = y_buf[phase, 0]
        for i in range(1, NY):
            total = total + y_buf[phase, i]
        return as_tile(total)

    to_sibling(0, jnp.sum(mixer * mixer, axis=1, keepdims=True))
    to_y(0)

    keys = NX * rows
    ahead = lax.broadcasted_iota(jnp.int32, (keys, rows), 1) - lax.broadcasted_iota(
        jnp.int32, (keys, rows), 0
    )

    def z_at(i):
        step = jnp.where(i % 2 == 1, (i + 1) // 2, NZ - i // 2)
        return lax.rem(z + step, NZ)

    def score_block(zp):
        allowed = ahead >= (z - zp) * keys - x * rows
        for h in range(heads):
            cols = slice(h * HEAD_DIM, (h + 1) * HEAD_DIM)
            scores = dot(k_all[:, cols], q_all[zp, :, cols], NT) * scale
            scores = jnp.where(allowed, scores, NEGATIVE)
            top = jnp.max(scores, axis=0, keepdims=True)
            total = jnp.sum(jnp.exp(scores - top), axis=0, keepdims=True)
            s_buf[zp * heads + h] = scores
            lse_buf[z, pl.ds(zp * heads + h, 1), :] = top + jnp.log(total)

    def score_step(i, carry):
        zp = z_at(i)
        arrive(q_all.at[zp], rq.at[zp], z_dev(zp))
        score_block(zp)
        return carry

    for o in x_order:
        xp = x_peer[o]
        arrive(k_all.at[pl.ds(pl.multiple_of(xp * rows, rows), rows)], rk.at[xp], x_dev(xp))
    score_block(z)
    split = min(3, NZ)
    lax.fori_loop(1, split, score_step, 0)

    inv = lax.rsqrt(from_y(0) / width + EPSILON)
    v_all[x_rows] = (mix_buf[...] * inv).astype(BF16)
    for o in x_order:
        push(v_all.at[x_rows], v_all.at[x_rows], rv.at[x], x_dev(x_peer[o]))

    lax.fori_loop(split, NZ, score_step, 0)
    for o in z_order:
        push(lse_buf.at[z], lse_buf.at[z], rlse.at[z], z_dev(z_peer[o]))

    for o in x_order:
        xp = x_peer[o]
        arrive(v_all.at[pl.ds(pl.multiple_of(xp * rows, rows), rows)], rv.at[xp], x_dev(xp))

    def dprob_block(zp):
        for h in range(heads):
            cols = slice(h * HEAD_DIM, (h + 1) * HEAD_DIM)
            dp_buf[zp * heads + h] = dot(v_all[:, cols], c_all[zp, :, cols], NT)

    def dprob_step(i, carry):
        zp = z_at(i)
        arrive(c_all.at[zp], rc.at[zp], z_dev(zp))
        dprob_block(zp)
        return carry

    dprob_block(z)
    lax.fori_loop(1, NZ, dprob_step, 0)

    for o in z_order:
        zp = z_peer[o]
        arrive(lse_buf.at[zp], rlse.at[zp], z_dev(zp))
    parts = lse_buf[...]
    top = jnp.max(parts, axis=0)
    lse_sum[...] = top + jnp.log(jnp.sum(jnp.exp(parts - top[None]), axis=0))

    def prob_block(zp, carry):
        for h in range(heads):
            row = zp * heads + h
            weights = jnp.exp(s_buf[row] - lse_sum[pl.ds(row, 1), :])
            s_buf[row] = weights
            p_low[h, :, pl.ds(pl.multiple_of(zp * rows, rows), rows)] = weights.astype(BF16)
            d_buf[z, pl.ds(row, 1), :] = jnp.sum(weights * dp_buf[row], axis=0, keepdims=True)
        return carry

    lax.fori_loop(0, NZ, prob_block, 0)
    for o in z_order:
        push(d_buf.at[z], d_buf.at[z], rd.at[z], z_dev(z_peer[o]))

    def columns(ref, h):
        cols = slice(h * HEAD_DIM, (h + 1) * HEAD_DIM)
        return ref[:, :, cols].reshape(NZ * rows, HEAD_DIM)

    for h in range(heads):
        cols = slice(h * HEAD_DIM, (h + 1) * HEAD_DIM)
        dv_src[:, cols] = dot(p_low[h], columns(c_all, h), NN).astype(BF16)
    for o in x_order:
        xp = x_peer[o]
        push(dv_src.at[pl.ds(pl.multiple_of(xp * rows, rows), rows)], dv_buf.at[x], rdv.at[x], x_dev(xp))
    dv_buf[x] = dv_src[x_rows]

    def across(src, low, ref):
        for h in range(heads):
            cols = slice(h * HEAD_DIM, (h + 1) * HEAD_DIM)
            full = dot(ref[:, cols], low[h], TN).astype(BF16)
            for i in range(NZ):
                src[i, cols, :] = full[:, i * rows : (i + 1) * rows]

    across(att_src, p_low, v_all)
    for o in z_order:
        zp = z_peer[o]
        push(att_src.at[zp], att_buf.at[z], ratt.at[z], z_dev(zp))
    att_buf[z] = att_src[z]

    for o in x_order:
        xp = x_peer[o]
        arrive(dv_buf.at[xp], rdv.at[xp], x_dev(xp))
    value_grad = dv_buf[0].astype(F32)
    for i in range(1, NX):
        value_grad = value_grad + dv_buf[i].astype(F32)
    to_sibling(1, jnp.sum(value_grad * mix_buf[...], axis=1, keepdims=True))
    to_y(1)

    for o in z_order:
        zp = z_peer[o]
        arrive(d_buf.at[zp], rd.at[zp], z_dev(zp))
    delta = d_buf[0]
    for i in range(1, NZ):
        delta = delta + d_buf[i]
    delta_sum[...] = delta

    def dscore_block(zp, carry):
        for h in range(heads):
            row = zp * heads + h
            dscore = s_buf[row] * (dp_buf[row] - delta_sum[pl.ds(row, 1), :])
            ds_low[h, :, pl.ds(pl.multiple_of(zp * rows, rows), rows)] = dscore.astype(BF16)
        return carry

    lax.fori_loop(0, NZ, dscore_block, 0)
    across(dq_src, ds_low, k_all)
    for o in z_order:
        zp = z_peer[o]
        push(dq_src.at[zp], dq_buf.at[z], rdq.at[z], z_dev(zp))
    dq_buf[z] = dq_src[z]
    for h in range(heads):
        cols = slice(h * HEAD_DIM, (h + 1) * HEAD_DIM)
        dk_src[:, cols] = dot(ds_low[h], columns(q_all, h), NN).astype(BF16)
    for o in x_order:
        xp = x_peer[o]
        push(dk_src.at[pl.ds(pl.multiple_of(xp * rows, rows), rows)], dk_buf.at[x], rdk.at[x], x_dev(xp))
    dk_buf[x] = dk_src[x_rows]

    proj = from_y(1)
    mixer_grad = inv * value_grad - mix_buf[...] * (inv * inv * inv * proj / width)
    ggo_o[...] = (mixer_grad * conv_buf[...]).astype(BF16)
    conv_grad = (mixer_grad * go[...].astype(F32)).astype(BF16)
    sums = []
    for g in range(groups):
        pairs = dot(jnp.where(lane_group == g, conv_grad.astype(F32), 0.0).astype(BF16), win_back[...], NT)
        pairs = pltpu.roll(pairs, 1, 1, stride=1, stride_axis=0)
        sums.append(jnp.sum(pairs[:, taps:], axis=0, keepdims=True))
    fx_buf[x] = jnp.concatenate(sums, axis=0)
    for o in x_order:
        push(fx_buf.at[x], fx_buf.at[x], rfx.at[x], x_dev(x_peer[o]))
    for o in x_order:
        xp = x_peer[o]
        arrive(fx_buf.at[xp], rfx.at[xp], x_dev(xp))
    total = fx_buf[0]
    for i in range(1, NX):
        total = total + fx_buf[i]
    fz_buf[z] = total
    for o in z_order:
        push(fz_buf.at[z], fz_buf.at[z], rfz.at[z], z_dev(z_peer[o]))

    def from_z(buf, sem, factor, out):
        for o in z_order:
            zp = z_peer[o]
            arrive(buf.at[zp], sem.at[zp], z_dev(zp))
        total = buf[0].astype(F32)
        for i in range(1, NZ):
            total = total + buf[i].astype(F32)
        for h in range(heads):
            cols = slice(h * HEAD_DIM, (h + 1) * HEAD_DIM)
            out[:, cols] = (total[cols].T * factor).astype(BF16)

    from_z(att_buf, ratt, 1.0, att_o)
    for o in x_order:
        xp = x_peer[o]
        arrive(dk_buf.at[xp], rdk.at[xp], x_dev(xp))
    key_grad = dk_buf[0].astype(F32)
    for i in range(1, NX):
        key_grad = key_grad + dk_buf[i].astype(F32)
    dk_o[...] = (key_grad * scale).astype(BF16)
    from_z(dq_buf, rdq, scale, dq_o)

    for o in z_order:
        zp = z_peer[o]
        arrive(fz_buf.at[zp], rfz.at[zp], z_dev(zp))
    total = fz_buf[0]
    for i in range(1, NZ):
        total = total + fz_buf[i]
    gf_o[...] = total

    for copy in sends:
        copy.wait_send()

    @pl.when(ctx < last)
    def _():
        pltpu.make_async_remote_copy(
            src_ref=win.at[pl.ds(rows, rows)], dst_ref=win.at[pl.ds(0, rows)],
            send_sem=ssem.at[ssem.shape[0] - 1], recv_sem=rhalo,
            device_id=(after, ch), device_id_type=MESH,
        ).wait_send()


def solution(mesh):
    NZ, NY = mesh.shape["ctx"] // NX, mesh.shape["ch"] // NC

    def on_device(go, gi, ci, filt, q, k, cot):
        rows, chans = go.shape
        groups, taps = filt.shape
        heads = chans // HEAD_DIM
        keys, stats = NX * rows, NZ * heads
        n_send = 4 * (NX - 1) + 6 * (NZ - 1) + 2 * NY + (NX - 1) + (NZ - 1) + 1
        vmem, sem = pltpu.VMEM, pltpu.SemaphoreType.DMA
        block = jax.ShapeDtypeStruct((rows, chans), BF16)
        return pl.pallas_call(
            functools.partial(kernel, NZ, NY),
            out_shape=[block] * 4 + [jax.ShapeDtypeStruct((groups, taps), F32)],
            in_specs=[pl.BlockSpec(memory_space=vmem)] * 7,
            out_specs=[pl.BlockSpec(memory_space=vmem)] * 5,
            scratch_shapes=[
                vmem((keys, chans), BF16), vmem((keys, chans), BF16),
                vmem((NZ, rows, chans), BF16), vmem((NZ, rows, chans), BF16),
                vmem((2 * rows, chans), BF16), vmem((groups * rows, 2 * taps), BF16),
                vmem((stats, keys, rows), F32), vmem((stats, keys, rows), F32),
                vmem((heads, keys, NZ * rows), BF16), vmem((heads, keys, NZ * rows), BF16),
                vmem((NZ, stats, rows), F32), vmem((NZ, stats, rows), F32),
                vmem((2, NC, 8, rows), F32), vmem((2, NY, 8, rows), F32),
                vmem((NX, groups, taps), F32), vmem((NZ, groups, taps), F32),
                vmem((keys, chans), BF16), vmem((NX, rows, chans), BF16),
                vmem((keys, chans), BF16), vmem((NX, rows, chans), BF16),
                vmem((NZ, chans, rows), BF16), vmem((NZ, chans, rows), BF16),
                vmem((NZ, chans, rows), BF16), vmem((NZ, chans, rows), BF16),
                vmem((rows, chans), F32), vmem((rows, chans), F32),
                vmem((2 * rows, chans), BF16), vmem((stats, rows), F32), vmem((stats, rows), F32),
                sem((n_send,)), sem((NX,)), sem((NX,)), sem((NZ,)), sem((NZ,)), sem, sem((NZ,)), sem((NZ,)),
                sem((2,)), sem((2, NY)), sem((NX,)), sem((NX,)), sem((NZ,)), sem((NZ,)), sem((NX,)), sem((NZ,)),
            ],
            compiler_params=pltpu.CompilerParams(
                collective_id=0, has_side_effects=True, vmem_limit_bytes=48 * 1024 * 1024
            ),
            name="hyena",
        )(go, gi, ci, filt, q, k, cot)

    block = P("ctx", "ch")
    return jax.shard_map(
        on_device,
        mesh=mesh,
        in_specs=(block, block, block, P("ch", None), block, block, block),
        out_specs=(block, block, block, block, P("ch", None)),
        check_vma=False,
    )
```

time: 552 us -> 81.4 us (0.15)
  the two profiles are of different devices: /device:TPU:24 before, /device:TPU:1 now
where the time goes in v1:
time: 81.4 us; the launch traced here: 80.1 us
  Pallas kernels  70.6 us (87%)
  local copies, waits for them, and re-layouts  8.83 us (11%)
    pallas_call x1, Pallas kernels, on_device(): pl.pallas_call(functools.partial(kernel, NZ, NY), out_shape=[block] * 4 +...  70.6 us
    unnamed x19, local copies, waits for them, and re-layouts  8.83 us

profile of v1, /device:TPU:1, one launch (start us, length us, event | category | flops | bytes accessed | tf_op | source)
XLA Modules:
  0.0 80.1 jit_solution(1015309632560197432)
XLA Ops:
  0.6 0.0 copy-start
  0.6 0.8 %copy-done = bf16[128,256]{1,0:T(8,128)(2,1)S(1)} copy-done((bf16[128,256]{1,0:T(8,128)(2,1)S(1)}, bf16[128,256]{1,0:T(8,128)(2,1)}, u32[]{:S(2)}) %copy-start) | copy-done | bytes 65560
  1.5 0.0 copy-start.1
  1.5 0.8 %copy-done.1 = bf16[128,256]{1,0:T(8,128)(2,1)S(1)} copy-done((bf16[128,256]{1,0:T(8,128)(2,1)S(1)}, bf16[128,256]{1,0:T(8,128)(2,1)}, u32[]{:S(2)}) %copy-start.1) | copy-done | bytes 65560
  2.3 0.0 copy-start.2
  2.3 0.8 %copy-done.2 = bf16[128,256]{1,0:T(8,128)(2,1)S(1)} copy-done((bf16[128,256]{1,0:T(8,128)(2,1)S(1)}, bf16[128,256]{1,0:T(8,128)(2,1)}, u32[]{:S(2)}) %copy-start.2) | copy-done | bytes 65560
  3.2 0.0 copy-start.3
  3.2 0.8 %copy-done.3 = bf16[128,256]{1,0:T(8,128)(2,1)S(1)} copy-done((bf16[128,256]{1,0:T(8,128)(2,1)S(1)}, bf16[128,256]{1,0:T(8,128)(2,1)}, u32[]{:S(2)}) %copy-start.3) | copy-done | bytes 65560
  4.0 0.0 copy-start.4
  4.0 0.8 %copy-done.4 = bf16[128,256]{1,0:T(8,128)(2,1)S(1)} copy-done((bf16[128,256]{1,0:T(8,128)(2,1)S(1)}, bf16[128,256]{1,0:T(8,128)(2,1)}, u32[]{:S(2)}) %copy-start.4) | copy-done | bytes 65560
  4.8 0.0 copy-start.5
  4.8 0.8 %copy-done.5 = bf16[128,256]{1,0:T(8,128)(2,1)S(1)} copy-done((bf16[128,256]{1,0:T(8,128)(2,1)S(1)}, bf16[128,256]{1,0:T(8,128)(2,1)}, u32[]{:S(2)}) %copy-start.5) | copy-done | bytes 65560
  5.7 0.0 copy-start.6
  5.7 0.7 copy-done.6
  6.4 70.6 %hyena.1 = (bf16[128,256]{1,0:T(8,128)(2,1)S(1)}, bf16[128,256]{1,0:T(8,128)(2,1)S(1)}, bf16[128,256]{1,0:T(8,128)(2,1)S(1)}, bf16[128,256]{1,0:T(8,128)(2,1)S(1)}, f32[16,128]{1,0:T(8,128)S(1)}) custom-call(bf16[128,256]{1,0:T(8,128)(2,1)S(1)} %copy-done, bf16[128,256]{1,0:T(8,128)(2,1)S(1)} %copy-done.1, bf16[128,256]{1,0:T(8,128)(2,1)S(1)} %copy-done.2, ...), custom_call_target="tpu_custom_call" | custom-call | tf_op jit(solution)/shard_map/hyena/pallas_call | solution.py:400
  77.0 0.6 copy.17
  77.6 0.6 copy.18
  78.3 0.6 copy.19
  78.9 0.6 copy.20
  79.5 0.6 copy.21
Async XLA Ops:
  0.6 0.8 %copy-start = (bf16[128,256]{1,0:T(8,128)(2,1)S(1)}, bf16[128,256]{1,0:T(8,128)(2,1)}, u32[]{:S(2)}) copy-start(bf16[128,256]{1,0:T(8,128)(2,1)} %go.1) | copy-start | bytes 196612
  1.5 0.8 %copy-start.1 = (bf16[128,256]{1,0:T(8,128)(2,1)S(1)}, bf16[128,256]{1,0:T(8,128)(2,1)}, u32[]{:S(2)}) copy-start(bf16[128,256]{1,0:T(8,128)(2,1)} %gi.1) | copy-start | bytes 196612
  2.3 0.8 %copy-start.2 = (bf16[128,256]{1,0:T(8,128)(2,1)S(1)}, bf16[128,256]{1,0:T(8,128)(2,1)}, u32[]{:S(2)}) copy-start(bf16[128,256]{1,0:T(8,128)(2,1)} %ci.1) | copy-start | bytes 196612
  3.2 0.8 %copy-start.3 = (bf16[128,256]{1,0:T(8,128)(2,1)S(1)}, bf16[128,256]{1,0:T(8,128)(2,1)}, u32[]{:S(2)}) copy-start(bf16[128,256]{1,0:T(8,128)(2,1)} %q.1) | copy-start | bytes 196612
  4.0 0.8 %copy-start.4 = (bf16[128,256]{1,0:T(8,128)(2,1)S(1)}, bf16[128,256]{1,0:T(8,128)(2,1)}, u32[]{:S(2)}) copy-start(bf16[128,256]{1,0:T(8,128)(2,1)} %k.1) | copy-start | bytes 196612
  4.8 0.8 %copy-start.5 = (bf16[128,256]{1,0:T(8,128)(2,1)S(1)}, bf16[128,256]{1,0:T(8,128)(2,1)}, u32[]{:S(2)}) copy-start(bf16[128,256]{1,0:T(8,128)(2,1)} %cot.1) | copy-start | bytes 196612
  5.7 0.7 copy-start.6

commit v2 on v1

v2 whole, which is shorter than its diff:
```python
import functools
import math

import jax
import jax.numpy as jnp
from jax import lax
from jax.experimental import pallas as pl
from jax.experimental.pallas import tpu as pltpu
from jax.sharding import PartitionSpec as P

MESH = pl.DeviceIdType.MESH
HEAD_DIM = 128
NEGATIVE = -1e30
EPSILON = 1e-05
VMEM_GRANT = 62 * 1024 * 1024
NX = 4
NC = 2
F32 = jnp.float32
BF16 = jnp.bfloat16

NT = (((1,), (1,)), ((), ()))
NN = (((1,), (0,)), ((), ()))
TN = (((0,), (0,)), ((), ()))


def dot(a, b, dims):
    return lax.dot_general(a, b, dims, preferred_element_type=F32)


def kernel(
    NZ, NY,
    go_h, gi_h, ci_h, filt_h, q_h, k_h, cot_h,
    att_h, dq_h, dk_h, ggo_h, gf_h,
    go, gi, ci, filt, win, win_back, toep, conv_buf, mix_buf,
    k0, v0, q0, c0, k1, v1, q1, c1,
    s0, dp0, s1, dp1, p0, ds0, p1, ds1,
    lse0_buf, d0_buf, lse0_sum, d0_sum, part1, lse1_buf, d1_buf,
    core_buf, y_buf, fx_buf, fz_buf,
    dv0_src, dk0_src, dv1_src, dk1_src, att0_src, dq0_src, att1_src, dq1_src,
    dv0_buf, dk0_buf, dv1_buf, dk1_buf, att0_buf, dq0_buf, att1_buf, dq1_buf,
    att_o, dq_o, dk_o, ggo_o, gf_o,
    rload, rstore, ssem, rx, rz, ry, rcore, rhalo, sz,
):
    rows, chans = go_h.shape
    groups, taps = filt_h.shape
    group_size = chans // groups
    width = chans * NY * NC
    scale = 1.0 / math.sqrt(HEAD_DIM)
    row_keys = NX * rows
    ctx, ch = lax.axis_index("ctx"), lax.axis_index("ch")
    z, x = ctx // NX, ctx % NX
    y, core = ch // NC, ch % NC
    last = NZ * NX - 1
    head0, head1 = slice(0, HEAD_DIM), slice(HEAD_DIM, 2 * HEAD_DIM)

    def z_dev(zp):
        return (zp * NX + x, ch)

    def x_dev(xp):
        return (z * NX + xp, ch)

    def y_dev(yp):
        return (ctx, yp * NC + core)

    sibling = (ctx, y * NC + (1 - core))
    near = lambda n: [o for d in range(1, n // 2 + 1) for o in dict.fromkeys((d, n - d))]
    z_peers = [lax.rem(z + o, NZ) for o in near(NZ)]
    x_peers = [lax.rem(x + o, NX) for o in near(NX)]
    y_peers = [lax.rem(y + o, NY) for o in near(NY)]
    before = (lax.rem(ctx + last, last + 1), ch)
    after = (lax.rem(ctx + 1, last + 1), ch)

    def block(i):
        return pl.ds(pl.multiple_of(i * rows, rows), rows)

    stores = []

    def store(src, dst):
        copy = pltpu.make_async_copy(src, dst, rstore.at[len(stores)])
        stores.append(copy)
        copy.start()

    def remote(src, dst, send_sem, recv_sem, dev):
        return pltpu.make_async_remote_copy(
            src_ref=src, dst_ref=dst, send_sem=send_sem, recv_sem=recv_sem, device_id=dev, device_id_type=MESH
        )

    sends = []

    def push(src, dst, recv_sem, dev):
        copy = remote(src, dst, ssem.at[len(sends)], recv_sem, dev)
        sends.append(copy)
        copy.start()

    def arrive(dst, recv_sem, dev):
        remote(dst, dst, ssem.at[0], recv_sem, dev).wait_recv()

    def push_x(t, src, dst):
        for xp in x_peers:
            push(src(xp), dst, rx.at[t, x], x_dev(xp))

    def arrive_x(t, dst):
        for xp in x_peers:
            arrive(dst(xp), rx.at[t, xp], x_dev(xp))

    def push_z(t, src, dst):
        for zp in z_peers:
            push(src, dst, rz.at[t, z], z_dev(zp))

    def arrive_z(t, dst):
        for zp in z_peers:
            arrive(dst(zp), rz.at[t, zp], z_dev(zp))

    def lower(fn, carry=0):
        return lax.fori_loop(1, z + 1, lambda d, c: fn(z - d, c), carry)

    def higher(fn, carry=0):
        return lax.fori_loop(1, NZ - z, lambda d, c: fn(z + d, c), carry)

    one_way = []

    def push_way(way, t, src, dst):
        def copy(zp):
            return remote(src(zp), dst, sz.at[t, zp], rz.at[t, z], z_dev(zp))

        def start(zp, c):
            copy(zp).start()
            return c

        def finish(zp, c):
            copy(zp).wait_send()
            return c

        way(start)
        one_way.append((way, finish))

    def arrive_way(way, t, dst):
        def wait(zp, c):
            arrive(dst(zp), rz.at[t, zp], z_dev(zp))
            return c

        way(wait)

    barrier = pltpu.get_barrier_semaphore()
    greet = [z_dev(p) for p in z_peers] + [x_dev(p) for p in x_peers] + [y_dev(p) for p in y_peers]
    greet += [sibling, before]
    for dev in greet:
        pl.semaphore_signal(barrier, inc=1, device_id=dev, device_id_type=MESH)

    own_x, own_z = block(x), block(z)
    loads = [
        pltpu.make_async_copy(src, dst, rload.at[i])
        for i, (src, dst) in enumerate([
            (gi_h, gi), (ci_h, ci),
            (k_h.at[:, head0], k0.at[own_x]), (q_h.at[:, head1], q1.at[own_x]),
            (k_h.at[:, head1], k1.at[own_z]), (q_h.at[:, head0], q0.at[own_z]),
            (cot_h.at[:, head1], c1.at[own_x]), (cot_h.at[:, head0], c0.at[own_z]),
            (filt_h, filt), (go_h, go),
        ])
    ]
    for load in loads:
        load.start()

    nothing = jnp.zeros((rows, HEAD_DIM), BF16)

    def clear_lower(zp, c):
        for ref in (q0, c0):
            ref[block(zp)] = nothing
        for ref in (dv1_buf, dk1_buf):
            ref[block(zp)] = nothing
        return c

    def clear_higher(zp, c):
        for ref in (k1, v1, att0_buf, dq0_buf):
            ref[block(zp)] = nothing
        return c

    for load in loads[:2]:
        load.wait()
    win[rows:] = (gi[...].astype(F32) * ci[...].astype(F32)).astype(BF16)
    lower(clear_lower)
    higher(clear_higher)
    for load in loads[2:]:
        load.wait()

    pl.semaphore_wait(barrier, len(greet))

    def halo(dev):
        return remote(win.at[pl.ds(rows, rows)], win.at[pl.ds(0, rows)], ssem.at[ssem.shape[0] - 1], rhalo, dev)

    @pl.when(ctx < last)
    def _():
        halo(after).start()

    push_way(higher, 0, lambda zp: k1.at[own_z], k1.at[own_z])
    push_way(lower, 1, lambda zp: q0.at[own_z], q0.at[own_z])
    push_x(0, lambda xp: k0.at[own_x], k0.at[own_x])
    push_x(1, lambda xp: q1.at[own_x], q1.at[own_x])
    push_way(lower, 2, lambda zp: c0.at[own_z], c0.at[own_z])
    push_x(2, lambda xp: c1.at[own_x], c1.at[own_x])

    flip = (
        lax.broadcasted_iota(jnp.int32, (taps, 2 * taps), 0)
        + lax.broadcasted_iota(jnp.int32, (taps, 2 * taps), 1)
        == taps
    ).astype(F32).astype(BF16)
    turned = dot(filt[...], flip, NN)
    for g in range(groups):
        spread = jnp.broadcast_to(turned[g : g + 1], (rows, 2 * taps))
        spread = pltpu.roll(spread, 0, 1, stride=1, stride_axis=0)
        toep[g * rows : (g + 1) * rows] = spread.astype(BF16)
    p0[...] = jnp.zeros_like(p0)
    ds0[...] = jnp.zeros_like(ds0)
    p1[...] = jnp.zeros_like(p1)
    ds1[...] = jnp.zeros_like(ds1)
    lse0_buf[z] = jnp.full((NZ, rows), NEGATIVE, F32)
    d0_buf[z] = jnp.zeros((NZ, rows), F32)
    part1[...] = jnp.full(part1.shape, NEGATIVE, F32)

    @pl.when(ctx > 0)
    def _():
        halo(before).wait_recv()

    @pl.when(ctx == 0)
    def _():
        win[:rows] = jnp.zeros((rows, chans), BF16)

    lane_group = lax.broadcasted_iota(jnp.int32, (rows, chans), 1) // group_size
    window = win[...]
    conv = jnp.zeros((rows, chans), F32)
    for g in range(groups):
        part = dot(toep[g * rows : (g + 1) * rows], window, NN)
        conv = jnp.where(lane_group == g, part, conv)
    conv_buf[...] = conv
    mixer = go[...].astype(F32) * conv
    mix_buf[...] = mixer

    def as_row(column):
        return jnp.broadcast_to(column, (rows, 128)).T[:8]

    def as_tile(row):
        tile = jnp.broadcast_to(row[0:1], (128, rows)).T
        return jnp.concatenate([tile] * (chans // 128), axis=1)

    def to_y(phase, column):
        core_buf[phase, core] = as_row(column)
        push(core_buf.at[phase, core], core_buf.at[phase, core], rcore.at[phase], sibling)
        arrive(core_buf.at[phase, 1 - core], rcore.at[phase], sibling)
        y_buf[phase, y] = core_buf[phase, 0] + core_buf[phase, 1]
        for yp in y_peers:
            push(y_buf.at[phase, y], y_buf.at[phase, y], ry.at[phase, y], y_dev(yp))

    def from_y(phase):
        for yp in y_peers:
            arrive(y_buf.at[phase, yp], ry.at[phase, yp], y_dev(yp))
        total = y_buf[phase, 0]
        for i in range(1, NY):
            total = total + y_buf[phase, i]
        return as_tile(total)

    to_y(0, jnp.sum(mixer * mixer, axis=1, keepdims=True))
    back = (
        lax.broadcasted_iota(jnp.int32, (2 * rows, 2 * rows), 0)
        + lax.broadcasted_iota(jnp.int32, (2 * rows, 2 * rows), 1)
        == 2 * rows - 1
    ).astype(F32).astype(BF16)
    win_back[...] = dot(back, window, NN).astype(BF16)

    def ahead(shape):
        return lax.broadcasted_iota(jnp.int32, shape, 1) - lax.broadcasted_iota(jnp.int32, shape, 0)

    def totals(scores):
        top = jnp.max(scores, axis=0, keepdims=True)
        return top + jnp.log(jnp.sum(jnp.exp(scores - top), axis=0, keepdims=True))

    def score0(zp):
        scores = dot(k0[...], q0[block(zp)], NT) * scale
        scores = jnp.where(ahead(scores.shape) >= (z - zp) * row_keys - x * rows, scores, NEGATIVE)
        s0[zp] = scores
        lse0_buf[z, pl.ds(zp, 1), :] = totals(scores)

    def score1(zp):
        scores = dot(k1[block(zp)], q1[...], NT) * scale
        scores = jnp.where(ahead(scores.shape) >= (zp - z) * row_keys + x * rows, scores, NEGATIVE)
        s1[zp] = scores
        part1[pl.ds(zp, 1), :] = totals(scores)

    def score0_step(zp, c):
        arrive(q0.at[block(zp)], rz.at[1, zp], z_dev(zp))
        score0(zp)
        return c

    def score1_step(zp, c):
        arrive(k1.at[block(zp)], rz.at[0, zp], z_dev(zp))
        score1(zp)
        return c

    arrive_x(0, lambda xp: k0.at[block(xp)])
    score0(z)
    arrive_x(1, lambda xp: q1.at[block(xp)])
    score1(z)

    inv = lax.rsqrt(from_y(0) / width + EPSILON)
    values = (mix_buf[...] * inv).astype(BF16)
    v0[own_x] = values[:, head0]
    v1[own_z] = values[:, head1]
    push_way(higher, 3, lambda zp: v1.at[own_z], v1.at[own_z])
    push_x(3, lambda xp: v0.at[own_x], v0.at[own_x])

    def as_rows(line):
        cut = [line[:, i * rows : (i + 1) * rows] for i in range(NX)]
        return jnp.concatenate(cut + [jnp.zeros((8 - NX, rows), F32)], axis=0)

    def as_line(table):
        return jnp.concatenate([table[i : i + 1] for i in range(NX)], axis=1)

    def log_sum(parts):
        top = jnp.max(parts, axis=0, keepdims=True)
        return (top + jnp.log(jnp.sum(jnp.exp(parts - top), axis=0, keepdims=True)))

    lower(score1_step)
    lse1_buf[x] = as_rows(log_sum(part1[...]))
    push_x(4, lambda xp: lse1_buf.at[x], lse1_buf.at[x])
    higher(score0_step)
    push_z(4, lse0_buf.at[z], lse0_buf.at[z])

    arrive_x(2, lambda xp: c1.at[block(xp)])
    arrive_x(4, lambda xp: lse1_buf.at[xp])
    lse1 = as_line(log_sum(lse1_buf[...])[0])

    def prob1(zp, c):
        weights = jnp.exp(s1[zp] - lse1)
        s1[zp] = weights
        low = weights.astype(BF16)
        p1[block(zp)] = low
        dv1_src[block(zp)] = dot(low, c1[...], NN).astype(BF16)
        return c

    prob1(z, 0)
    lower(prob1)
    push_way(lower, 5, lambda zp: dv1_src.at[block(zp)], dv1_buf.at[own_z])
    dv1_buf[own_z] = dv1_src[own_z]

    arrive_way(higher, 2, lambda zp: c0.at[block(zp)])
    arrive_z(4, lambda zp: lse0_buf.at[zp])
    lse0_sum[...] = log_sum(lse0_buf[...])[0]

    def prob0(zp, c):
        weights = jnp.exp(s0[zp] - lse0_sum[pl.ds(zp, 1), :])
        s0[zp] = weights
        p0[:, block(zp)] = weights.astype(BF16)
        return c

    prob0(z, 0)
    higher(prob0)
    dv0_src[...] = dot(p0[...], c0[...], NN).astype(BF16)
    push_x(5, lambda xp: dv0_src.at[block(xp)], dv0_buf.at[own_x])
    dv0_buf[own_x] = dv0_src[own_x]

    def dprob1(zp, total):
        dprob = dot(v1[block(zp)], c1[...], NT)
        dp1[zp] = dprob
        return total + jnp.sum(s1[zp] * dprob, axis=0, keepdims=True)

    def dprob0(zp, c):
        dprob = dot(v0[...], c0[block(zp)], NT)
        dp0[zp] = dprob
        d0_buf[z, pl.ds(zp, 1), :] = jnp.sum(s0[zp] * dprob, axis=0, keepdims=True)
        return c

    arrive_x(3, lambda xp: v0.at[block(xp)])
    dprob0(z, 0)
    higher(dprob0)
    push_z(6, d0_buf.at[z], d0_buf.at[z])

    arrive_way(lower, 3, lambda zp: v1.at[block(zp)])
    d1_buf[x] = as_rows(lower(dprob1, dprob1(z, jnp.zeros((1, row_keys), F32))))
    push_x(6, lambda xp: d1_buf.at[x], d1_buf.at[x])

    def across(src, keys, low, count):
        full = dot(keys[...], low[...], TN).astype(BF16)
        for i in range(count):
            src[i * HEAD_DIM : (i + 1) * HEAD_DIM] = full[:, i * rows : (i + 1) * rows]

    across(att0_src, v0, p0, NZ)
    push_way(higher, 7, lambda zp: att0_src.at[block(zp)], att0_buf.at[own_z])
    att0_buf[own_z] = att0_src[own_z]
    across(att1_src, v1, p1, NX)
    push_x(7, lambda xp: att1_src.at[block(xp)], att1_buf.at[own_x])
    att1_buf[own_x] = att1_src[own_x]

    def added(ref, count):
        total = ref[:rows].astype(F32)
        for i in range(1, count):
            total = total + ref[i * rows : (i + 1) * rows].astype(F32)
        return total

    arrive_way(higher, 5, lambda zp: dv1_buf.at[block(zp)])
    arrive_x(5, lambda xp: dv0_buf.at[block(xp)])
    value_grad = jnp.concatenate([added(dv0_buf, NX), added(dv1_buf, NZ)], axis=1)
    to_y(1, jnp.sum(value_grad * mix_buf[...], axis=1, keepdims=True))

    arrive_z(6, lambda zp: d0_buf.at[zp])
    delta0 = d0_buf[0]
    for i in range(1, NZ):
        delta0 = delta0 + d0_buf[i]
    d0_sum[...] = delta0

    def dscore0(zp, c):
        dscore = s0[zp] * (dp0[zp] - d0_sum[pl.ds(zp, 1), :])
        ds0[:, block(zp)] = dscore.astype(BF16)
        return c

    dscore0(z, 0)
    higher(dscore0)
    across(dq0_src, k0, ds0, NZ)
    push_way(higher, 8, lambda zp: dq0_src.at[block(zp)], dq0_buf.at[own_z])
    dq0_buf[own_z] = dq0_src[own_z]

    arrive_x(6, lambda xp: d1_buf.at[xp])
    delta1 = d1_buf[0]
    for i in range(1, NX):
        delta1 = delta1 + d1_buf[i]
    delta1 = as_line(delta1)

    def dscore1(zp, c):
        low = (s1[zp] * (dp1[zp] - delta1)).astype(BF16)
        ds1[block(zp)] = low
        dk1_src[block(zp)] = dot(low, q1[...], NN).astype(BF16)
        return c

    dscore1(z, 0)
    lower(dscore1)
    push_way(lower, 9, lambda zp: dk1_src.at[block(zp)], dk1_buf.at[own_z])
    dk1_buf[own_z] = dk1_src[own_z]
    dk0_src[...] = dot(ds0[...], q0[...], NN).astype(BF16)
    push_x(8, lambda xp: dk0_src.at[block(xp)], dk0_buf.at[own_x])
    dk0_buf[own_x] = dk0_src[own_x]
    across(dq1_src, k1, ds1, NX)
    push_x(9, lambda xp: dq1_src.at[block(xp)], dq1_buf.at[own_x])
    dq1_buf[own_x] = dq1_src[own_x]

    proj = from_y(1)
    mixer_grad = inv * value_grad - mix_buf[...] * (inv * inv * inv * proj / width)
    ggo_o[...] = (mixer_grad * conv_buf[...]).astype(BF16)
    store(ggo_o, ggo_h)
    conv_grad = (mixer_grad * go[...].astype(F32)).astype(BF16).astype(F32)
    sums = []
    for g in range(groups):
        pairs = dot(jnp.where(lane_group == g, conv_grad, 0.0).astype(BF16), win_back[...], NT)
        pairs = pltpu.roll(pairs, 1, 1, stride=1, stride_axis=0)
        sums.append(jnp.sum(pairs[:, taps:], axis=0, keepdims=True))
    fx_buf[x] = jnp.concatenate(sums, axis=0)
    push_x(10, lambda xp: fx_buf.at[x], fx_buf.at[x])
    arrive_x(10, lambda xp: fx_buf.at[xp])
    total = fx_buf[0]
    for i in range(1, NX):
        total = total + fx_buf[i]
    fz_buf[z] = total
    push_z(10, fz_buf.at[z], fz_buf.at[z])

    arrive_x(7, lambda xp: att1_buf.at[block(xp)])
    att_o[:, head1] = added(att1_buf, NX).T.astype(BF16)
    arrive_way(lower, 7, lambda zp: att0_buf.at[block(zp)])
    att_o[:, head0] = added(att0_buf, NZ).T.astype(BF16)
    store(att_o, att_h)
    arrive_x(8, lambda xp: dk0_buf.at[block(xp)])
    dk_o[:, head0] = (added(dk0_buf, NX) * scale).astype(BF16)
    arrive_way(higher, 9, lambda zp: dk1_buf.at[block(zp)])
    dk_o[:, head1] = (added(dk1_buf, NZ) * scale).astype(BF16)
    store(dk_o, dk_h)
    arrive_x(9, lambda xp: dq1_buf.at[block(xp)])
    dq_o[:, head1] = (added(dq1_buf, NX).T * scale).astype(BF16)
    arrive_way(lower, 8, lambda zp: dq0_buf.at[block(zp)])
    dq_o[:, head0] = (added(dq0_buf, NZ).T * scale).astype(BF16)
    store(dq_o, dq_h)

    arrive_z(10, lambda zp: fz_buf.at[zp])
    total = fz_buf[0]
    for i in range(1, NZ):
        total = total + fz_buf[i]
    gf_o[...] = total
    store(gf_o, gf_h)

    for copy in sends:
        copy.wait_send()
    for way, finish in one_way:
        way(finish)
    for copy in stores:
        copy.wait()

    @pl.when(ctx < last)
    def _():
        halo(after).wait_send()


def write_out(*refs):
    held, sems = refs[10:15], refs[15]
    loads = [pltpu.make_async_copy(refs[i], held[i], sems.at[i]) for i in range(5)]
    stores = [pltpu.make_async_copy(held[i], refs[5 + i], sems.at[5 + i]) for i in range(5)]
    for load in loads:
        load.start()
    for load, store in zip(loads, stores):
        load.wait()
        store.start()
    for store in stores:
        store.wait()


def solution(mesh):
    NZ, NY = mesh.shape["ctx"] // NX, mesh.shape["ch"] // NC

    def on_device(go, gi, ci, filt, q, k, cot):
        rows, chans = go.shape
        groups, taps = filt.shape
        along_x, along_z = NX * rows, NZ * rows
        n_send = 11 * (NX - 1) + 3 * (NZ - 1) + 2 * NY + 1
        vmem, sem = pltpu.VMEM, pltpu.SemaphoreType.DMA
        block = jax.ShapeDtypeStruct((rows, chans), BF16)
        outs = [block] * 4 + [jax.ShapeDtypeStruct((groups, taps), F32)]
        own = vmem((rows, chans), BF16)
        row_x, row_z = vmem((along_x, HEAD_DIM), BF16), vmem((along_z, HEAD_DIM), BF16)
        results = pl.pallas_call(
            functools.partial(kernel, NZ, NY),
            out_shape=outs,
            in_specs=[pl.BlockSpec(memory_space=pltpu.HBM)] * 7,
            out_specs=[pl.BlockSpec(memory_space=pltpu.HBM)] * 5,
            scratch_shapes=[
                own, own, own, vmem((groups, taps), BF16),
                vmem((2 * rows, chans), BF16), vmem((2 * rows, chans), BF16), vmem((groups * rows, 2 * taps), BF16),
                vmem((rows, chans), F32), vmem((rows, chans), F32),
                row_x, row_x, row_z, row_z, row_z, row_z, row_x, row_x,
                vmem((NZ, along_x, rows), F32), vmem((NZ, along_x, rows), F32),
                vmem((NZ, rows, along_x), F32), vmem((NZ, rows, along_x), F32),
                vmem((along_x, along_z), BF16), vmem((along_x, along_z), BF16),
                vmem((along_z, along_x), BF16), vmem((along_z, along_x), BF16),
                vmem((NZ, NZ, rows), F32), vmem((NZ, NZ, rows), F32), vmem((NZ, rows), F32), vmem((NZ, rows), F32),
                vmem((NZ, along_x), F32), vmem((NX, 8, rows), F32), vmem((NX, 8, rows), F32),
                vmem((2, NC, 8, rows), F32), vmem((2, NY, 8, rows), F32),
                vmem((NX, groups, taps), F32), vmem((NZ, groups, taps), F32),
                row_x, row_x, row_z, row_z, row_z, row_z, row_x, row_x,
                row_x, row_x, row_z, row_z, row_z, row_z, row_x, row_x,
                own, own, own, own, vmem((groups, taps), F32),
                sem((10,)), sem((5,)), sem((n_send,)), sem((11, NX)), sem((11, NZ)), sem((2, NY)), sem((2,)), sem,
                sem((11, NZ)),
            ],
            compiler_params=pltpu.CompilerParams(
                collective_id=0, has_side_effects=True, vmem_limit_bytes=VMEM_GRANT
            ),
            name="hyena",
        )(go, gi, ci, filt, q, k, cot)
        return pl.pallas_call(
            write_out,
            out_shape=outs,
            in_specs=[pl.BlockSpec(memory_space=pltpu.HBM)] * 5,
            out_specs=[pl.BlockSpec(memory_space=pltpu.HBM)] * 5,
            scratch_shapes=[vmem(o.shape, o.dtype) for o in outs] + [sem((10,))],
            compiler_params=pltpu.CompilerParams(vmem_limit_bytes=VMEM_GRANT),
            name="write_out",
        )(*results)

    block = P("ctx", "ch")
    return jax.shard_map(
        on_device,
        mesh=mesh,
        in_specs=(block, block, block, P("ch", None), block, block, block),
        out_specs=(block, block, block, block, P("ch", None)),
        check_vma=False,
    )
```

time: 81.4 us -> 62.1 us (0.76)
  Pallas kernels: 70.6 us -> 60.5 us
  local copies, waits for them, and re-layouts: 8.83 us -> 0 us
    pallas_call x1 -> x2, Pallas kernels: 70.6 us -> 60.5 us  [the longest x1 58.9 us: on_device(): pl.pallas_call(functools.partial(kernel, NZ, NY), out_shape=outs, in_spec...]
    unnamed x19 -> x0, local copies, waits for them, and re-layouts: 8.83 us -> none
where the time goes in v2:
time: 62.1 us; the launch traced here: 61.2 us
  Pallas kernels  60.5 us (97%)
  between operations  0.64 us (1%)
    pallas_call x1, Pallas kernels, on_device(): pl.pallas_call(functools.partial(kernel, NZ, NY), out_shape=outs, in_spec...  58.9 us
    pallas_call x1, Pallas kernels, on_device(): pl.pallas_call(write_out, out_shape=outs, in_specs=[pl.BlockSpec(memory_s...  1.65 us

profile of v2, /device:TPU:1, one launch (start us, length us, event | category | flops | bytes accessed | tf_op | source)
XLA Modules:
  0.0 61.2 jit_solution(4083417295609684670)
XLA Ops:
  0.6 58.9 %hyena.1 = (bf16[128,256]{1,0:T(8,128)(2,1)}, bf16[128,256]{1,0:T(8,128)(2,1)}, bf16[128,256]{1,0:T(8,128)(2,1)}, bf16[128,256]{1,0:T(8,128)(2,1)}, f32[16,128]{1,0:T(8,128)}) custom-call(bf16[128,256]{1,0:T(8,128)(2,1)} %go_h.1, bf16[128,256]{1,0:T(8,128)(2,1)} %gi_h.1, bf16[128,256]{1,0:T(8,128)(2,1)} %ci_h.1, bf16[16,128]{1,0:T(8,128)(2,1)} %filt_h.1, ...), custom_call_target="tpu_custom_call" | custom-call | tf_op jit(solution)/shard_map/hyena/pallas_call | solution.py:523
  59.5 1.7 %write_out.1 = (bf16[128,256]{1,0:T(8,128)(2,1)}, bf16[128,256]{1,0:T(8,128)(2,1)}, bf16[128,256]{1,0:T(8,128)(2,1)}, bf16[128,256]{1,0:T(8,128)(2,1)}, f32[16,128]{1,0:T(8,128)}) custom-call(bf16[128,256]{1,0:T(8,128)(2,1)} %get-tuple-element.10.refs_0_, bf16[128,256]{1,0:T(8,128)(2,1)} %get-tuple-element.11.refs_1_, ...), custom_call_target="tpu_custom_call" | custom-call | tf_op jit(solution)/shard_map/write_out/pallas_call | solution.py:552

commit v3 on v2

--- a/solution.py
+++ b/solution.py
@@ -34,7 +34,7 @@
     go, gi, ci, filt, win, win_back, toep, conv_buf, mix_buf,
     k0, v0, q0, c0, k1, v1, q1, c1,
     s0, dp0, s1, dp1, p0, ds0, p1, ds1,
-    lse0_buf, d0_buf, lse0_sum, d0_sum, part1, lse1_buf, d1_buf,
+    lse0_buf, d0_buf, lse0_sum, d0_sum, top0, top1, part1, lse1_buf, d1_buf,
     core_buf, y_buf, fx_buf, fz_buf,
     dv0_src, dk0_src, dv1_src, dk1_src, att0_src, dq0_src, att1_src, dq1_src,
     dv0_buf, dk0_buf, dv1_buf, dk1_buf, att0_buf, dq0_buf, att1_buf, dq1_buf,
@@ -209,14 +209,20 @@
         spread = jnp.broadcast_to(turned[g : g + 1], (rows, 2 * taps))
         spread = pltpu.roll(spread, 0, 1, stride=1, stride_axis=0)
         toep[g * rows : (g + 1) * rows] = spread.astype(BF16)
-    p0[...] = jnp.zeros_like(p0)
-    ds0[...] = jnp.zeros_like(ds0)
-    p1[...] = jnp.zeros_like(p1)
-    ds1[...] = jnp.zeros_like(ds1)
     lse0_buf[z] = jnp.full((NZ, rows), NEGATIVE, F32)
     d0_buf[z] = jnp.zeros((NZ, rows), F32)
     part1[...] = jnp.full(part1.shape, NEGATIVE, F32)
 
+    lane_group = lax.broadcasted_iota(jnp.int32, (rows, chans), 1) // group_size
+
+    def conv_part(conv, cols, tokens):
+        for g in range(groups):
+            part = dot(toep[g * rows : (g + 1) * rows, cols], tokens, NN)
+            conv = conv + jnp.where(lane_group == g, part, 0.0)
+        return conv
+
+    conv_buf[...] = conv_part(jnp.zeros((rows, chans), F32), slice(rows, 2 * rows), win[rows:])
+
     @pl.when(ctx > 0)
     def _():
         halo(before).wait_recv()
@@ -225,12 +231,7 @@
     def _():
         win[:rows] = jnp.zeros((rows, chans), BF16)
 
-    lane_group = lax.broadcasted_iota(jnp.int32, (rows, chans), 1) // group_size
-    window = win[...]
-    conv = jnp.zeros((rows, chans), F32)
-    for g in range(groups):
-        part = dot(toep[g * rows : (g + 1) * rows], window, NN)
-        conv = jnp.where(lane_group == g, part, conv)
+    conv = conv_part(conv_buf[...], slice(0, rows), win[:rows])
     conv_buf[...] = conv
     mixer = go[...].astype(F32) * conv
     mix_buf[...] = mixer
@@ -245,6 +246,8 @@
     def to_y(phase, column):
         core_buf[phase, core] = as_row(column)
         push(core_buf.at[phase, core], core_buf.at[phase, core], rcore.at[phase], sibling)
+
+    def on_to_y(phase):
         arrive(core_buf.at[phase, 1 - core], rcore.at[phase], sibling)
         y_buf[phase, y] = core_buf[phase, 0] + core_buf[phase, 1]
         for yp in y_peers:
@@ -259,31 +262,31 @@
         return as_tile(total)
 
     to_y(0, jnp.sum(mixer * mixer, axis=1, keepdims=True))
+    on_to_y(0)
     back = (
         lax.broadcasted_iota(jnp.int32, (2 * rows, 2 * rows), 0)
         + lax.broadcasted_iota(jnp.int32, (2 * rows, 2 * rows), 1)
         == 2 * rows - 1
     ).astype(F32).astype(BF16)
-    win_back[...] = dot(back, window, NN).astype(BF16)
+    win_back[...] = dot(back, win[...], NN).astype(BF16)
 
     def ahead(shape):
         return lax.broadcasted_iota(jnp.int32, shape, 1) - lax.broadcasted_iota(jnp.int32, shape, 0)
 
     def totals(scores):
         top = jnp.max(scores, axis=0, keepdims=True)
-        return top + jnp.log(jnp.sum(jnp.exp(scores - top), axis=0, keepdims=True))
+        powers = jnp.exp(scores - top)
+        return top, powers, top + jnp.log(jnp.sum(powers, axis=0, keepdims=True))
 
     def score0(zp):
         scores = dot(k0[...], q0[block(zp)], NT) * scale
         scores = jnp.where(ahead(scores.shape) >= (z - zp) * row_keys - x * rows, scores, NEGATIVE)
-        s0[zp] = scores
-        lse0_buf[z, pl.ds(zp, 1), :] = totals(scores)
+        top0[pl.ds(zp, 1), :], s0[zp], lse0_buf[z, pl.ds(zp, 1), :] = totals(scores)
 
     def score1(zp):
         scores = dot(k1[block(zp)], q1[...], NT) * scale
         scores = jnp.where(ahead(scores.shape) >= (zp - z) * row_keys + x * rows, scores, NEGATIVE)
-        s1[zp] = scores
-        part1[pl.ds(zp, 1), :] = totals(scores)
+        top1[pl.ds(zp, 1), :], s1[zp], part1[pl.ds(zp, 1), :] = totals(scores)
 
     def score0_step(zp, c):
         arrive(q0.at[block(zp)], rz.at[1, zp], z_dev(zp))
@@ -299,6 +302,23 @@
     score0(z)
     arrive_x(1, lambda xp: q1.at[block(xp)])
     score1(z)
+
+    def as_rows(line):
+        cut = [line[:, i * rows : (i + 1) * rows] for i in range(NX)]
+        return jnp.concatenate(cut + [jnp.zeros((8 - NX, rows), F32)], axis=0)
+
+    def as_line(table):
+        return jnp.concatenate([table[i : i + 1] for i in range(NX)], axis=1)
+
+    def log_sum(parts):
+        top = jnp.max(parts, axis=0, keepdims=True)
+        return (top + jnp.log(jnp.sum(jnp.exp(parts - top), axis=0, keepdims=True)))
+
+    lower(score1_step)
+    lse1_buf[x] = as_rows(log_sum(part1[...]))
+    push_x(4, lambda xp: lse1_buf.at[x], lse1_buf.at[x])
+    higher(score0_step)
+    push_z(4, lse0_buf.at[z], lse0_buf.at[z])
 
     inv = lax.rsqrt(from_y(0) / width + EPSILON)
     values = (mix_buf[...] * inv).astype(BF16)
@@ -307,29 +327,25 @@
     push_way(higher, 3, lambda zp: v1.at[own_z], v1.at[own_z])
     push_x(3, lambda xp: v0.at[own_x], v0.at[own_x])
 
-    def as_rows(line):
-        cut = [line[:, i * rows : (i + 1) * rows] for i in range(NX)]
-        return jnp.concatenate(cut + [jnp.zeros((8 - NX, rows), F32)], axis=0)
-
-    def as_line(table):
-        return jnp.concatenate([table[i : i + 1] for i in range(NX)], axis=1)
-
-    def log_sum(parts):
-        top = jnp.max(parts, axis=0, keepdims=True)
-        return (top + jnp.log(jnp.sum(jnp.exp(parts - top), axis=0, keepdims=True)))
-
-    lower(score1_step)
-    lse1_buf[x] = as_rows(log_sum(part1[...]))
-    push_x(4, lambda xp: lse1_buf.at[x], lse1_buf.at[x])
-    higher(score0_step)
-    push_z(4, lse0_buf.at[z], lse0_buf.at[z])
+    def clear_columns(zp, c):
+        p0[:, block(zp)] = jnp.zeros((row_keys, rows), BF16)
+        ds0[:, block(zp)] = jnp.zeros((row_keys, rows), BF16)
+        return c
+
+    def clear_rows(zp, c):
+        p1[block(zp)] = jnp.zeros((rows, row_keys), BF16)
+        ds1[block(zp)] = jnp.zeros((rows, row_keys), BF16)
+        return c
+
+    lower(clear_columns)
+    higher(clear_rows)
 
     arrive_x(2, lambda xp: c1.at[block(xp)])
     arrive_x(4, lambda xp: lse1_buf.at[xp])
     lse1 = as_line(log_sum(lse1_buf[...])[0])
 
     def prob1(zp, c):
-        weights = jnp.exp(s1[zp] - lse1)
+        weights = s1[zp] * jnp.exp(top1[pl.ds(zp, 1), :] - lse1)
         s1[zp] = weights
         low = weights.astype(BF16)
         p1[block(zp)] = low
@@ -346,7 +362,7 @@
     lse0_sum[...] = log_sum(lse0_buf[...])[0]
 
     def prob0(zp, c):
-        weights = jnp.exp(s0[zp] - lse0_sum[pl.ds(zp, 1), :])
+        weights = s0[zp] * jnp.exp(top0[pl.ds(zp, 1), :] - lse0_sum[pl.ds(zp, 1), :])
         s0[zp] = weights
         p0[:, block(zp)] = weights.astype(BF16)
         return c
@@ -385,9 +401,6 @@
     across(att0_src, v0, p0, NZ)
     push_way(higher, 7, lambda zp: att0_src.at[block(zp)], att0_buf.at[own_z])
     att0_buf[own_z] = att0_src[own_z]
-    across(att1_src, v1, p1, NX)
-    push_x(7, lambda xp: att1_src.at[block(xp)], att1_buf.at[own_x])
-    att1_buf[own_x] = att1_src[own_x]
 
     def added(ref, count):
         total = ref[:rows].astype(F32)
@@ -399,6 +412,10 @@
     arrive_x(5, lambda xp: dv0_buf.at[block(xp)])
     value_grad = jnp.concatenate([added(dv0_buf, NX), added(dv1_buf, NZ)], axis=1)
     to_y(1, jnp.sum(value_grad * mix_buf[...], axis=1, keepdims=True))
+    across(att1_src, v1, p1, NX)
+    push_x(7, lambda xp: att1_src.at[block(xp)], att1_buf.at[own_x])
+    att1_buf[own_x] = att1_src[own_x]
+    on_to_y(1)
 
     arrive_z(6, lambda zp: d0_buf.at[zp])
     delta0 = d0_buf[0]
@@ -442,28 +459,28 @@
 
     proj = from_y(1)
     mixer_grad = inv * value_grad - mix_buf[...] * (inv * inv * inv * proj / width)
-    ggo_o[...] = (mixer_grad * conv_buf[...]).astype(BF16)
-    store(ggo_o, ggo_h)
     conv_grad = (mixer_grad * go[...].astype(F32)).astype(BF16).astype(F32)
     sums = []
     for g in range(groups):
         pairs = dot(jnp.where(lane_group == g, conv_grad, 0.0).astype(BF16), win_back[...], NT)
         pairs = pltpu.roll(pairs, 1, 1, stride=1, stride_axis=0)
         sums.append(jnp.sum(pairs[:, taps:], axis=0, keepdims=True))
-    fx_buf[x] = jnp.concatenate(sums, axis=0)
+    fx_buf[x] = jnp.concatenate(sums, axis=0).astype(BF16)
     push_x(10, lambda xp: fx_buf.at[x], fx_buf.at[x])
-    arrive_x(10, lambda xp: fx_buf.at[xp])
-    total = fx_buf[0]
-    for i in range(1, NX):
-        total = total + fx_buf[i]
-    fz_buf[z] = total
-    push_z(10, fz_buf.at[z], fz_buf.at[z])
-
+    ggo_o[...] = (mixer_grad * conv_buf[...]).astype(BF16)
+    store(ggo_o, ggo_h)
     arrive_x(7, lambda xp: att1_buf.at[block(xp)])
     att_o[:, head1] = added(att1_buf, NX).T.astype(BF16)
     arrive_way(lower, 7, lambda zp: att0_buf.at[block(zp)])
     att_o[:, head0] = added(att0_buf, NZ).T.astype(BF16)
     store(att_o, att_h)
+    arrive_x(10, lambda xp: fx_buf.at[xp])
+    total = fx_buf[0].astype(F32)
+    for i in range(1, NX):
+        total = total + fx_buf[i].astype(F32)
+    fz_buf[z] = total.astype(BF16)
+    push_z(10, fz_buf.at[z], fz_buf.at[z])
+
     arrive_x(8, lambda xp: dk0_buf.at[block(xp)])
     dk_o[:, head0] = (added(dk0_buf, NX) * scale).astype(BF16)
     arrive_way(higher, 9, lambda zp: dk1_buf.at[block(zp)])
@@ -476,9 +493,9 @@
     store(dq_o, dq_h)
 
     arrive_z(10, lambda zp: fz_buf.at[zp])
-    total = fz_buf[0]
+    total = fz_buf[0].astype(F32)
     for i in range(1, NZ):
-        total = total + fz_buf[i]
+        total = total + fz_buf[i].astype(F32)
     gf_o[...] = total
     store(gf_o, gf_h)
 
@@ -535,9 +552,9 @@
                 vmem((along_x, along_z), BF16), vmem((along_x, along_z), BF16),
                 vmem((along_z, along_x), BF16), vmem((along_z, along_x), BF16),
                 vmem((NZ, NZ, rows), F32), vmem((NZ, NZ, rows), F32), vmem((NZ, rows), F32), vmem((NZ, rows), F32),
-                vmem((NZ, along_x), F32), vmem((NX, 8, rows), F32), vmem((NX, 8, rows), F32),
+                vmem((NZ, rows), F32), vmem((NZ, along_x), F32), vmem((NZ, along_x), F32), vmem((NX, 8, rows), F32), vmem((NX, 8, rows), F32),
                 vmem((2, NC, 8, rows), F32), vmem((2, NY, 8, rows), F32),
-                vmem((NX, groups, taps), F32), vmem((NZ, groups, taps), F32),
+                vmem((NX, groups, taps), BF16), vmem((NZ, groups, taps), BF16),
                 row_x, row_x, row_z, row_z, row_z, row_z, row_x, row_x,
                 row_x, row_x, row_z, row_z, row_z, row_z, row_x, row_x,
                 own, own, own, own, vmem((groups, taps), F32),

time: 62.1 us -> 58.3 us (0.939); the launches traced: 61.2 us -> 58.1 us
  Pallas kernels: 60.5 us -> 57.4 us
    pallas_call x1, Pallas kernels: 58.9 us -> 55.8 us  [on_device(): pl.pallas_call(functools.partial(kernel, NZ, NY), out_shape=outs, in_spec...]
where the time goes in v3:
time: 58.3 us; the launch traced here: 58.1 us
  Pallas kernels  57.4 us (98%)
  between operations  0.64 us (1%)
    pallas_call x1, Pallas kernels, on_device(): pl.pallas_call(functools.partial(kernel, NZ, NY), out_shape=outs, in_spec...  55.8 us
    pallas_call x1, Pallas kernels, on_device(): pl.pallas_call(write_out, out_shape=outs, in_specs=[pl.BlockSpec(memory_s...  1.65 us

profile of v3, /device:TPU:1, one launch (start us, length us, event | category | flops | bytes accessed | tf_op | source)
XLA Modules:
  0.0 58.1 jit_solution(17810018949017309368)
XLA Ops:
  0.6 55.8 %hyena.1 = (bf16[128,256]{1,0:T(8,128)(2,1)}, bf16[128,256]{1,0:T(8,128)(2,1)}, bf16[128,256]{1,0:T(8,128)(2,1)}, bf16[128,256]{1,0:T(8,128)(2,1)}, f32[16,128]{1,0:T(8,128)}) custom-call(bf16[128,256]{1,0:T(8,128)(2,1)} %go_h.1, bf16[128,256]{1,0:T(8,128)(2,1)} %gi_h.1, bf16[128,256]{1,0:T(8,128)(2,1)} %ci_h.1, bf16[16,128]{1,0:T(8,128)(2,1)} %filt_h.1, ...), custom_call_target="tpu_custom_call" | custom-call | tf_op jit(solution)/shard_map/hyena/pallas_call | solution.py:540
  56.4 1.7 %write_out.1 = (bf16[128,256]{1,0:T(8,128)(2,1)}, bf16[128,256]{1,0:T(8,128)(2,1)}, bf16[128,256]{1,0:T(8,128)(2,1)}, bf16[128,256]{1,0:T(8,128)(2,1)}, f32[16,128]{1,0:T(8,128)}) custom-call(bf16[128,256]{1,0:T(8,128)(2,1)} %get-tuple-element.10.refs_0_, bf16[128,256]{1,0:T(8,128)(2,1)} %get-tuple-element.11.refs_1_, ...), custom_call_target="tpu_custom_call" | custom-call | tf_op jit(solution)/shard_map/write_out/pallas_call | solution.py:569

commit v4 on v3

--- a/solution.py
+++ b/solution.py
@@ -39,7 +39,7 @@
     dv0_src, dk0_src, dv1_src, dk1_src, att0_src, dq0_src, att1_src, dq1_src,
     dv0_buf, dk0_buf, dv1_buf, dk1_buf, att0_buf, dq0_buf, att1_buf, dq1_buf,
     att_o, dq_o, dk_o, ggo_o, gf_o,
-    rload, rstore, ssem, rx, rz, ry, rcore, rhalo, sz,
+    rload, rstore, sx, rx, sz, rz, sz_all, rz_all, sy, ry, score, rcore, shalo, rhalo,
 ):
     rows, chans = go_h.shape
     groups, taps = filt_h.shape
@@ -85,31 +85,27 @@
             src_ref=src, dst_ref=dst, send_sem=send_sem, recv_sem=recv_sem, device_id=dev, device_id_type=MESH
         )
 
-    sends = []
-
-    def push(src, dst, recv_sem, dev):
-        copy = remote(src, dst, ssem.at[len(sends)], recv_sem, dev)
-        sends.append(copy)
-        copy.start()
+    ends = []
+
+    def push(peers, dev, src, dst, send_sem, recv_sem, all_sent):
+        for p in peers:
+            remote(src(p), dst, send_sem, recv_sem, dev(p)).start()
+        ends.append(lambda: remote(all_sent, all_sent, send_sem, recv_sem, dev(peers[0])).wait_send())
 
     def arrive(dst, recv_sem, dev):
-        remote(dst, dst, ssem.at[0], recv_sem, dev).wait_recv()
-
-    def push_x(t, src, dst):
-        for xp in x_peers:
-            push(src(xp), dst, rx.at[t, x], x_dev(xp))
-
-    def arrive_x(t, dst):
-        for xp in x_peers:
-            arrive(dst(xp), rx.at[t, xp], x_dev(xp))
-
-    def push_z(t, src, dst):
-        for zp in z_peers:
-            push(src, dst, rz.at[t, z], z_dev(zp))
-
-    def arrive_z(t, dst):
-        for zp in z_peers:
-            arrive(dst(zp), rz.at[t, zp], z_dev(zp))
+        remote(dst, dst, sx.at[0], recv_sem, dev).wait_recv()
+
+    def push_x(t, src, dst, some):
+        push(x_peers, x_dev, src, dst, sx.at[t], rx.at[t], some)
+
+    def arrive_x(t, some):
+        arrive(some, rx.at[t], x_dev(x_peers[0]))
+
+    def push_z(t, src, dst, some):
+        push(z_peers, z_dev, src, dst, sz_all.at[t], rz_all.at[t], some)
+
+    def arrive_z(t, some):
+        arrive(some, rz_all.at[t], z_dev(z_peers[0]))
 
     def lower(fn, carry=0):
         return lax.fori_loop(1, z + 1, lambda d, c: fn(z - d, c), carry)
@@ -148,6 +144,7 @@
         pl.semaphore_signal(barrier, inc=1, device_id=dev, device_id_type=MESH)
 
     own_x, own_z = block(x), block(z)
+    most_x = pl.ds(0, (NX - 1) * rows)
     loads = [
         pltpu.make_async_copy(src, dst, rload.at[i])
         for i, (src, dst) in enumerate([
@@ -186,7 +183,7 @@
     pl.semaphore_wait(barrier, len(greet))
 
     def halo(dev):
-        return remote(win.at[pl.ds(rows, rows)], win.at[pl.ds(0, rows)], ssem.at[ssem.shape[0] - 1], rhalo, dev)
+        return remote(win.at[pl.ds(rows, rows)], win.at[pl.ds(0, rows)], shalo, rhalo, dev)
 
     @pl.when(ctx < last)
     def _():
@@ -194,10 +191,10 @@
 
     push_way(higher, 0, lambda zp: k1.at[own_z], k1.at[own_z])
     push_way(lower, 1, lambda zp: q0.at[own_z], q0.at[own_z])
-    push_x(0, lambda xp: k0.at[own_x], k0.at[own_x])
-    push_x(1, lambda xp: q1.at[own_x], q1.at[own_x])
+    push_x(0, lambda xp: k0.at[own_x], k0.at[own_x], k0.at[most_x])
+    push_x(1, lambda xp: q1.at[own_x], q1.at[own_x], q1.at[most_x])
     push_way(lower, 2, lambda zp: c0.at[own_z], c0.at[own_z])
-    push_x(2, lambda xp: c1.at[own_x], c1.at[own_x])
+    push_x(2, lambda xp: c1.at[own_x], c1.at[own_x], c1.at[most_x])
 
     flip = (
         lax.broadcasted_iota(jnp.int32, (taps, 2 * taps), 0)
@@ -245,17 +242,17 @@
 
     def to_y(phase, column):
         core_buf[phase, core] = as_row(column)
-        push(core_buf.at[phase, core], core_buf.at[phase, core], rcore.at[phase], sibling)
+        own = core_buf.at[phase, core]
+        push([0], lambda p: sibling, lambda p: own, own, score.at[phase], rcore.at[phase], own)
 
     def on_to_y(phase):
         arrive(core_buf.at[phase, 1 - core], rcore.at[phase], sibling)
         y_buf[phase, y] = core_buf[phase, 0] + core_buf[phase, 1]
-        for yp in y_peers:
-            push(y_buf.at[phase, y], y_buf.at[phase, y], ry.at[phase, y], y_dev(yp))
+        own = y_buf.at[phase, y]
+        push(y_peers, y_dev, lambda p: own, own, sy.at[phase], ry.at[phase], y_buf.at[phase, pl.ds(0, NY - 1)])
 
     def from_y(phase):
-        for yp in y_peers:
-            arrive(y_buf.at[phase, yp], ry.at[phase, yp], y_dev(yp))
+        arrive(y_buf.at[phase, pl.ds(0, NY - 1)], ry.at[phase], y_dev(y_peers[0]))
         total = y_buf[phase, 0]
         for i in range(1, NY):
             total = total + y_buf[phase, i]
@@ -298,9 +295,9 @@
         score1(zp)
         return c
 
-    arrive_x(0, lambda xp: k0.at[block(xp)])
+    arrive_x(0, k0.at[most_x])
     score0(z)
-    arrive_x(1, lambda xp: q1.at[block(xp)])
+    arrive_x(1, q1.at[most_x])
     score1(z)
 
     def as_rows(line):
@@ -316,16 +313,16 @@
 
     lower(score1_step)
     lse1_buf[x] = as_rows(log_sum(part1[...]))
-    push_x(4, lambda xp: lse1_buf.at[x], lse1_buf.at[x])
+    push_x(4, lambda xp: lse1_buf.at[x], lse1_buf.at[x], lse1_buf.at[pl.ds(0, NX - 1)])
     higher(score0_step)
-    push_z(4, lse0_buf.at[z], lse0_buf.at[z])
+    push_z(0, lambda zp: lse0_buf.at[z], lse0_buf.at[z], lse0_buf.at[pl.ds(0, NZ - 1)])
 
     inv = lax.rsqrt(from_y(0) / width + EPSILON)
     values = (mix_buf[...] * inv).astype(BF16)
     v0[own_x] = values[:, head0]
     v1[own_z] = values[:, head1]
     push_way(higher, 3, lambda zp: v1.at[own_z], v1.at[own_z])
-    push_x(3, lambda xp: v0.at[own_x], v0.at[own_x])
+    push_x(3, lambda xp: v0.at[own_x], v0.at[own_x], v0.at[most_x])
 
     def clear_columns(zp, c):
         p0[:, block(zp)] = jnp.zeros((row_keys, rows), BF16)
@@ -340,8 +337,8 @@
     lower(clear_columns)
     higher(clear_rows)
 
-    arrive_x(2, lambda xp: c1.at[block(xp)])
-    arrive_x(4, lambda xp: lse1_buf.at[xp])
+    arrive_x(2, c1.at[most_x])
+    arrive_x(4, lse1_buf.at[pl.ds(0, NX - 1)])
     lse1 = as_line(log_sum(lse1_buf[...])[0])
 
     def prob1(zp, c):
@@ -358,7 +355,7 @@
     dv1_buf[own_z] = dv1_src[own_z]
 
     arrive_way(higher, 2, lambda zp: c0.at[block(zp)])
-    arrive_z(4, lambda zp: lse0_buf.at[zp])
+    arrive_z(0, lse0_buf.at[pl.ds(0, NZ - 1)])
     lse0_sum[...] = log_sum(lse0_buf[...])[0]
 
     def prob0(zp, c):
@@ -370,7 +367,7 @@
     prob0(z, 0)
     higher(prob0)
     dv0_src[...] = dot(p0[...], c0[...], NN).astype(BF16)
-    push_x(5, lambda xp: dv0_src.at[block(xp)], dv0_buf.at[own_x])
+    push_x(5, lambda xp: dv0_src.at[block(xp)], dv0_buf.at[own_x], dv0_buf.at[most_x])
     dv0_buf[own_x] = dv0_src[own_x]
 
     def dprob1(zp, total):
@@ -384,14 +381,14 @@
         d0_buf[z, pl.ds(zp, 1), :] = jnp.sum(s0[zp] * dprob, axis=0, keepdims=True)
         return c
 
-    arrive_x(3, lambda xp: v0.at[block(xp)])
+    arrive_x(3, v0.at[most_x])
     dprob0(z, 0)
     higher(dprob0)
-    push_z(6, d0_buf.at[z], d0_buf.at[z])
+    push_z(1, lambda zp: d0_buf.at[z], d0_buf.at[z], d0_buf.at[pl.ds(0, NZ - 1)])
 
     arrive_way(lower, 3, lambda zp: v1.at[block(zp)])
     d1_buf[x] = as_rows(lower(dprob1, dprob1(z, jnp.zeros((1, row_keys), F32))))
-    push_x(6, lambda xp: d1_buf.at[x], d1_buf.at[x])
+    push_x(6, lambda xp: d1_buf.at[x], d1_buf.at[x], d1_buf.at[pl.ds(0, NX - 1)])
 
     def across(src, keys, low, count):
         full = dot(keys[...], low[...], TN).astype(BF16)
@@ -409,15 +406,15 @@
         return total
 
     arrive_way(higher, 5, lambda zp: dv1_buf.at[block(zp)])
-    arrive_x(5, lambda xp: dv0_buf.at[block(xp)])
+    arrive_x(5, dv0_buf.at[most_x])
     value_grad = jnp.concatenate([added(dv0_buf, NX), added(dv1_buf, NZ)], axis=1)
     to_y(1, jnp.sum(value_grad * mix_buf[...], axis=1, keepdims=True))
     across(att1_src, v1, p1, NX)
-    push_x(7, lambda xp: att1_src.at[block(xp)], att1_buf.at[own_x])
+    push_x(7, lambda xp: att1_src.at[block(xp)], att1_buf.at[own_x], att1_buf.at[most_x])
     att1_buf[own_x] = att1_src[own_x]
     on_to_y(1)
 
-    arrive_z(6, lambda zp: d0_buf.at[zp])
+    arrive_z(1, d0_buf.at[pl.ds(0, NZ - 1)])
     delta0 = d0_buf[0]
     for i in range(1, NZ):
         delta0 = delta0 + d0_buf[i]
@@ -434,7 +431,7 @@
     push_way(higher, 8, lambda zp: dq0_src.at[block(zp)], dq0_buf.at[own_z])
     dq0_buf[own_z] = dq0_src[own_z]
 
-    arrive_x(6, lambda xp: d1_buf.at[xp])
+    arrive_x(6, d1_buf.at[pl.ds(0, NX - 1)])
     delta1 = d1_buf[0]
     for i in range(1, NX):
         delta1 = delta1 + d1_buf[i]
@@ -451,10 +448,10 @@
     push_way(lower, 9, lambda zp: dk1_src.at[block(zp)], dk1_buf.at[own_z])
     dk1_buf[own_z] = dk1_src[own_z]
     dk0_src[...] = dot(ds0[...], q0[...], NN).astype(BF16)
-    push_x(8, lambda xp: dk0_src.at[block(xp)], dk0_buf.at[own_x])
+    push_x(8, lambda xp: dk0_src.at[block(xp)], dk0_buf.at[own_x], dk0_buf.at[most_x])
     dk0_buf[own_x] = dk0_src[own_x]
     across(dq1_src, k1, ds1, NX)
-    push_x(9, lambda xp: dq1_src.at[block(xp)], dq1_buf.at[own_x])
+    push_x(9, lambda xp: dq1_src.at[block(xp)], dq1_buf.at[own_x], dq1_buf.at[most_x])
     dq1_buf[own_x] = dq1_src[own_x]
 
     proj = from_y(1)
@@ -466,49 +463,52 @@
         pairs = pltpu.roll(pairs, 1, 1, stride=1, stride_axis=0)
         sums.append(jnp.sum(pairs[:, taps:], axis=0, keepdims=True))
     fx_buf[x] = jnp.concatenate(sums, axis=0).astype(BF16)
-    push_x(10, lambda xp: fx_buf.at[x], fx_buf.at[x])
+    push_x(10, lambda xp: fx_buf.at[x], fx_buf.at[x], fx_buf.at[pl.ds(0, NX - 1)])
     ggo_o[...] = (mixer_grad * conv_buf[...]).astype(BF16)
     store(ggo_o, ggo_h)
-    arrive_x(7, lambda xp: att1_buf.at[block(xp)])
+    arrive_x(7, att1_buf.at[most_x])
     att_o[:, head1] = added(att1_buf, NX).T.astype(BF16)
     arrive_way(lower, 7, lambda zp: att0_buf.at[block(zp)])
     att_o[:, head0] = added(att0_buf, NZ).T.astype(BF16)
     store(att_o, att_h)
-    arrive_x(10, lambda xp: fx_buf.at[xp])
+    arrive_x(10, fx_buf.at[pl.ds(0, NX - 1)])
     total = fx_buf[0].astype(F32)
     for i in range(1, NX):
         total = total + fx_buf[i].astype(F32)
     fz_buf[z] = total.astype(BF16)
-    push_z(10, fz_buf.at[z], fz_buf.at[z])
-
-    arrive_x(8, lambda xp: dk0_buf.at[block(xp)])
+    early = list(ends)
+    push_z(2, lambda zp: fz_buf.at[z], fz_buf.at[z], fz_buf.at[pl.ds(0, NZ - 1)])
+
+    arrive_x(8, dk0_buf.at[most_x])
     dk_o[:, head0] = (added(dk0_buf, NX) * scale).astype(BF16)
     arrive_way(higher, 9, lambda zp: dk1_buf.at[block(zp)])
     dk_o[:, head1] = (added(dk1_buf, NZ) * scale).astype(BF16)
     store(dk_o, dk_h)
-    arrive_x(9, lambda xp: dq1_buf.at[block(xp)])
+    arrive_x(9, dq1_buf.at[most_x])
     dq_o[:, head1] = (added(dq1_buf, NX).T * scale).astype(BF16)
     arrive_way(lower, 8, lambda zp: dq0_buf.at[block(zp)])
     dq_o[:, head0] = (added(dq0_buf, NZ).T * scale).astype(BF16)
     store(dq_o, dq_h)
 
-    arrive_z(10, lambda zp: fz_buf.at[zp])
+    for end in early:
+        end()
+    for way, finish in one_way:
+        way(finish)
+
+    @pl.when(ctx < last)
+    def _():
+        halo(after).wait_send()
+
+    arrive_z(2, fz_buf.at[pl.ds(0, NZ - 1)])
     total = fz_buf[0].astype(F32)
     for i in range(1, NZ):
         total = total + fz_buf[i].astype(F32)
     gf_o[...] = total
     store(gf_o, gf_h)
 
-    for copy in sends:
-        copy.wait_send()
-    for way, finish in one_way:
-        way(finish)
+    ends[-1]()
     for copy in stores:
         copy.wait()
-
-    @pl.when(ctx < last)
-    def _():
-        halo(after).wait_send()
 
 
 def write_out(*refs):
@@ -531,7 +531,6 @@
         rows, chans = go.shape
         groups, taps = filt.shape
         along_x, along_z = NX * rows, NZ * rows
-        n_send = 11 * (NX - 1) + 3 * (NZ - 1) + 2 * NY + 1
         vmem, sem = pltpu.VMEM, pltpu.SemaphoreType.DMA
         block = jax.ShapeDtypeStruct((rows, chans), BF16)
         outs = [block] * 4 + [jax.ShapeDtypeStruct((groups, taps), F32)]
@@ -558,8 +557,8 @@
                 row_x, row_x, row_z, row_z, row_z, row_z, row_x, row_x,
                 row_x, row_x, row_z, row_z, row_z, row_z, row_x, row_x,
                 own, own, own, own, vmem((groups, taps), F32),
-                sem((10,)), sem((5,)), sem((n_send,)), sem((11, NX)), sem((11, NZ)), sem((2, NY)), sem((2,)), sem,
-                sem((11, NZ)),
+                sem((10,)), sem((5,)), sem((11,)), sem((11,)), sem((10, NZ)), sem((10, NZ)), sem((3,)), sem((3,)),
+                sem((2,)), sem((2,)), sem((2,)), sem((2,)), sem, sem,
             ],
             compiler_params=pltpu.CompilerParams(
                 collective_id=0, has_side_effects=True, vmem_limit_bytes=VMEM_GRANT

time: 58.3 us -> 57.2 us (0.981)
  Pallas kernels: 57.4 us -> 56.4 us
    pallas_call x1, Pallas kernels: 55.8 us -> 54.7 us  [on_device(): pl.pallas_call(functools.partial(kernel, NZ, NY), out_shape=outs, in_spec...]
where the time goes in v4:
time: 57.2 us; the launch traced here: 57 us
  Pallas kernels  56.4 us (99%)
  between operations  0.64 us (1%)
    pallas_call x1, Pallas kernels, on_device(): pl.pallas_call(functools.partial(kernel, NZ, NY), out_shape=outs, in_spec...  54.7 us
    pallas_call x1, Pallas kernels, on_device(): pl.pallas_call(write_out, out_shape=outs, in_specs=[pl.BlockSpec(memory_s...  1.65 us

profile of v4, /device:TPU:1, one launch (start us, length us, event | category | flops | bytes accessed | tf_op | source)
XLA Modules:
  0.0 57.0 jit_solution(11000396985030661925)
XLA Ops:
  0.6 54.7 %hyena.1 = (bf16[128,256]{1,0:T(8,128)(2,1)}, bf16[128,256]{1,0:T(8,128)(2,1)}, bf16[128,256]{1,0:T(8,128)(2,1)}, bf16[128,256]{1,0:T(8,128)(2,1)}, f32[16,128]{1,0:T(8,128)}) custom-call(bf16[128,256]{1,0:T(8,128)(2,1)} %go_h.1, bf16[128,256]{1,0:T(8,128)(2,1)} %gi_h.1, bf16[128,256]{1,0:T(8,128)(2,1)} %ci_h.1, bf16[16,128]{1,0:T(8,128)(2,1)} %filt_h.1, ...), custom_call_target="tpu_custom_call" | custom-call | tf_op jit(solution)/shard_map/hyena/pallas_call | solution.py:539
  55.4 1.7 %write_out.1 = (bf16[128,256]{1,0:T(8,128)(2,1)}, bf16[128,256]{1,0:T(8,128)(2,1)}, bf16[128,256]{1,0:T(8,128)(2,1)}, bf16[128,256]{1,0:T(8,128)(2,1)}, f32[16,128]{1,0:T(8,128)}) custom-call(bf16[128,256]{1,0:T(8,128)(2,1)} %get-tuple-element.10.refs_0_, bf16[128,256]{1,0:T(8,128)(2,1)} %get-tuple-element.11.refs_1_, ...), custom_call_target="tpu_custom_call" | custom-call | tf_op jit(solution)/shard_map/write_out/pallas_call | solution.py:568
